TPU v7x, 256 devices: a whole 4x4x8 slice. The times are simulated.
256 devices in a mesh: dp: 16 (over y, x), ctx: 16 (over z, core).
Axes of the slice: x: 4, y: 4, z: 8, core: 2. Of those that a mesh axis runs over, the one named last changes fastest.
Arguments:
- hidden_in: bfloat16 [16, 3072, 16384], P('dp', 'ctx'), may hold values from -8 to 8
- queries: bfloat16 [16, 3072, 1024], P('dp', 'ctx'), may hold values from -14 to 14
- grad_out: bfloat16 [16, 3072, 1024], P('dp', 'ctx'), may hold values from -6 to 6
- w_key: bfloat16 [16384, 128], P('dp'), may hold values from -1 to 1
- w_value: bfloat16 [16384, 128], P('dp'), may hold values from -0.046875 to 0.046875
- stretch_order: int32 [32], replicated, may hold values from 0 to 31, each once
- doc_lengths: int32 [16, 8], P('dp'), may hold values from 1 to 1536, 3072 in all within a row
Outputs:
- query_grad: bfloat16 [16, 3072, 1024], P('dp', 'ctx')
- key_weight_grad: float32 [16384, 128], P('dp')
- value_weight_grad: float32 [16384, 128], P('dp')
Inputs may be any that keep to these rules, and one draw needn't show every extreme that they name: `stretch_order`: every block number appears exactly once. `doc_lengths`: each sequence's lengths sum to 3072, and one of them is 1536.
All inputs are finite; a program needn't handle non-finite values.
Results may differ from a plain program's by a relative error of at most 0.03.
Values may be sent and summed in bfloat16 or wider, within the bound.
A program may use at most 128 MiB of HBM per device.

v0:
```python
import math

import jax
import jax.numpy as jnp
from jax import lax
from jax.sharding import PartitionSpec as P


def table_lookup(slots, table):
    choices_all = jnp.arange(table.shape[0], dtype=jnp.int32)
    return jnp.sum(jnp.where(slots[:, None] == choices_all[None, :], table[None, :], 0), axis=1)


def place_and_doc(stored, stretch_order, stretch_rows, doc_ends):
    place = (
        table_lookup(stored // stretch_rows, stretch_order) * stretch_rows + stored % stretch_rows
    )
    documents = jnp.sum((place[:, None] >= doc_ends[None, :]).astype(jnp.int32), axis=1)
    return (place, documents)


def attention_grads(query_rows, key_rows, value_rows, cotangent, allowed, head_count, head_dim):
    row_count = query_rows.shape[0]
    score_scale = 1.0 / math.sqrt(head_dim)
    query_heads = jnp.transpose(query_rows.reshape(row_count, head_count, head_dim), (1, 0, 2))
    cot_heads = jnp.transpose(cotangent.reshape(row_count, head_count, head_dim), (1, 0, 2))

    def one_head(running, items):
        query_one, cot_one = items
        scores = (
            jnp.dot(query_one, jnp.transpose(key_rows), preferred_element_type=jnp.float32)
            * score_scale
        )
        masked = jnp.where(allowed, scores, -jnp.inf)
        row_max = jnp.max(masked, axis=-1, keepdims=True)
        expsum = jnp.where(allowed, jnp.exp(masked - row_max), 0.0)
        probabilities = expsum / jnp.sum(expsum, axis=-1, keepdims=True)
        probs_low = probabilities.astype(jnp.bfloat16)
        attended = jnp.dot(probs_low, value_rows, preferred_element_type=jnp.float32)
        delta_rows = jnp.sum(cot_one.astype(jnp.float32) * attended, axis=-1)
        dprob = jnp.dot(cot_one, jnp.transpose(value_rows), preferred_element_type=jnp.float32)
        dscore = (probabilities * (dprob - delta_rows[:, None])).astype(jnp.bfloat16)
        query_grad = (
            jnp.dot(dscore, key_rows, preferred_element_type=jnp.float32) * score_scale
        ).astype(jnp.bfloat16)
        key_grad = (
            lax.dot_general(
                dscore, query_one, (((0,), (0,)), ((), ())), preferred_element_type=jnp.float32
            )
            * score_scale
        )
        value_grad = lax.dot_general(
            probs_low, cot_one, (((0,), (0,)), ((), ())), preferred_element_type=jnp.float32
        )
        return (running + jnp.concatenate([key_grad, value_grad], axis=1), query_grad)

    start_sum = jnp.zeros((key_rows.shape[0], 2 * head_dim), jnp.float32)
    kv_grads, query_grad = lax.scan(one_head, start_sum, (query_heads, cot_heads))
    return (
        jnp.transpose(query_grad, (1, 0, 2)).reshape(row_count, head_count * head_dim),
        kv_grads,
    )


def on_device(hidden_in, queries, grad_out, w_key, w_value, stretch_order, doc_lengths):
    inputs = hidden_in[0]
    row_count = inputs.shape[0]
    stretch_rows = row_count // 2
    head_dim = w_key.shape[1]
    head_count = queries.shape[2] // head_dim
    ctx_count = lax.axis_size("ctx")
    seq_rows = row_count * ctx_count
    stacked = jnp.concatenate([w_key, w_value], axis=1)
    columns = inputs
    projected = jnp.dot(
        columns,
        lax.all_gather(stacked, "dp", axis=0, tiled=True),
        preferred_element_type=jnp.float32,
    ).astype(jnp.bfloat16)
    gathered = lax.all_gather(projected, "ctx", axis=0, tiled=True)
    doc_ends = jnp.cumsum(doc_lengths[0])
    every_row = jnp.arange(seq_rows, dtype=jnp.int32)
    own_rows = lax.axis_index("ctx") * row_count + jnp.arange(row_count, dtype=jnp.int32)
    key_place, key_docs = place_and_doc(every_row, stretch_order, stretch_rows, doc_ends)
    query_place, query_docs = place_and_doc(own_rows, stretch_order, stretch_rows, doc_ends)
    allowed = (key_place[None, :] <= query_place[:, None]) & (
        key_docs[None, :] == query_docs[:, None]
    )
    query_grad, kv_partial = attention_grads(
        queries[0],
        gathered[:, :head_dim],
        gathered[:, head_dim:],
        grad_out[0],
        allowed,
        head_count,
        head_dim,
    )
    kv_grads = lax.psum_scatter(
        kv_partial.astype(jnp.bfloat16), "ctx", scatter_dimension=0, tiled=True
    )
    columns = inputs
    partial_rows = lax.psum_scatter(
        lax.dot_general(
            columns, kv_grads, (((0,), (0,)), ((), ())), preferred_element_type=jnp.float32
        ).astype(jnp.bfloat16),
        "dp",
        scatter_dimension=0,
        tiled=True,
    )
    weight_grads = lax.psum(partial_rows, "ctx").astype(jnp.float32)
    return (
        query_grad.reshape(1, row_count, head_count * head_dim),
        weight_grads[:, :head_dim],
        weight_grads[:, head_dim:],
    )


def solution(mesh):
    return jax.shard_map(
        on_device,
        mesh=mesh,
        in_specs=(
            P("dp", "ctx", None),
            P("dp", "ctx", None),
            P("dp", "ctx", None),
            P("dp", None),
            P("dp", None),
            P(),
            P("dp", None),
        ),
        out_specs=(P("dp", "ctx", None), P("dp", None), P("dp", None)),
        check_vma=False,
    )
```

profile of v0, /device:TPU:1, one launch (start us, length us, event | category | flops | bytes accessed | tf_op | source)
XLA Modules:
  0.0 494.5 jit_solution(5097747195582043551)
XLA Ops:
  7.2 1.9 pad_maximum_fusion
  9.2 81.4 %all-gather.3.cloned.1.call-done = bf16[16384,256]{1,0:T(8,128)(2,1)} async-done(((bf16[1024,256]{1,0:T(8,128)(2,1)}), bf16[16384,256]{1,0:T(8,128)(2,1)}) %all-gather.3.cloned.1.call-update) | async-done | bytes 8388624 | tf_op jit(solution)/shard_map/all_gather | solution.py:77
  90.6 7.6 %fusion.33 = bf16[192,256]{1,0:T(8,128)(2,1)} fusion(bf16[16384,256]{1,0:T(8,128)(2,1)} %all-gather.3.cloned.1.call-done, bf16[1,192,16384]{2,1,0:T(8,128)(2,1)} %param.9), kind=kOutput, calls=%fused_computation.39 | convolution fusion | flops 1610661888 | bytes 14778368 | tf_op jit(solution)/shard_map/dot_general | solution.py:75
  99.1 0.8 copy.23
  99.9 1.1 copy.31
  101.2 1.3 convert_reduce_fusion.1
  102.5 0.8 select_reduce_fusion
  103.3 1.3 convert_reduce_fusion
  104.6 33.1 %all-gather.5.cloned.1.call-done = bf16[3072,256]{1,0:T(8,128)(2,1)} async-done(((bf16[192,256]{1,0:T(8,128)(2,1)}), bf16[3072,256]{1,0:T(8,128)(2,1)}) %all-gather.5.cloned.1.call-update) | async-done | bytes 1572880 | tf_op jit(solution)/shard_map/all_gather | solution.py:80
  137.7 2.6 fusion.48
  140.3 75.2 %while.13 = (s32[]{:T(128)}, f32[3072,256]{0,1:T(8,128)S(1)}, bf16[8,192,128]{2,1,0:T(8,128)(2,1)}, bf16[8,192,128]{2,1,0:T(8,128)(2,1)}, bf16[3072,128]{1,0:T(8...) while((s32[]{:T(128)}, f32[3072,256]{0,1:T(8,128)S(1)}, ...), condition=%wide.region_9.10_spmd.clone, body=%wide.region_5.9_spmd.clone.sunk | while | flops 922410432 | bytes 42505748 | solution.py:58
  140.3 1.9 fusion.87
  143.0 0.8 fusion.89
  146.3 1.1 fusion.93
  147.4 1.2 convolution_multiply_fusion.5
  148.6 1.1 maximum_add_fusion.2
  149.7 1.9 fusion.87
  151.6 0.8 fusion.88
  152.4 0.8 fusion.89
  155.7 1.1 fusion.93
  156.8 1.2 convolution_multiply_fusion.5
  158.0 1.1 maximum_add_fusion.2
  159.1 1.9 fusion.87
  161.0 0.8 fusion.88
  161.8 0.8 fusion.89
  165.1 1.1 fusion.93
  166.2 1.2 convolution_multiply_fusion.5
  167.4 1.1 maximum_add_fusion.2
  168.5 1.9 fusion.87
  170.4 0.8 fusion.88
  171.2 0.8 fusion.89
  174.5 1.1 fusion.93
  175.6 1.2 convolution_multiply_fusion.5
  176.8 1.1 maximum_add_fusion.2
  177.9 1.9 fusion.87
  180.6 0.8 fusion.89
  183.9 1.1 fusion.93
  185.0 1.2 convolution_multiply_fusion.5
  186.2 1.1 maximum_add_fusion.2
  187.3 1.9 fusion.87
  190.0 0.8 fusion.89
  193.3 1.1 fusion.93
  194.4 1.2 convolution_multiply_fusion.5
  195.6 1.1 maximum_add_fusion.2
  196.7 1.9 fusion.87
  199.4 0.8 fusion.89
  202.7 1.1 fusion.93
  203.8 1.2 convolution_multiply_fusion.5
  205.0 1.1 maximum_add_fusion.2
  206.1 1.9 fusion.87
  208.8 0.8 fusion.89
  212.1 1.1 fusion.93
  213.2 1.2 convolution_multiply_fusion.5
  214.4 1.1 maximum_add_fusion.2
  215.5 1.4 convert_element_type.40
  216.8 2.6 copy.28
  219.5 53.6 %reduce-scatter.7.cloned.1.call-done = bf16[192,256]{1,0:T(8,128)(2,1)} async-done(((bf16[3072,256]{1,0:T(8,128)(2,1)}), bf16[192,256]{1,0:T(8,128)(2,1)}) %reduce-scatter.7.cloned.1.call-update) | async-done | bytes 98320
  273.1 8.4 %fusion.26 = bf16[16384,256]{0,1:T(8,128)(2,1)} fusion(bf16[192,256]{1,0:T(8,128)(2,1)} %reduce-scatter.7.cloned.1.call-done, bf16[1,192,16384]{2,1,0:T(8,128)(2,1)} %param.9), kind=kOutput, calls=%fused_computation.34 | convolution fusion | flops 1614807040 | bytes 14778368 | tf_op jit(solution)/shard_map/dot_general | solution.py:103
  281.7 90.6 %reduce-scatter.5.cloned.1.call-done = bf16[1024,256]{0,1:T(8,128)(2,1)} async-done(((bf16[16384,256]{0,1:T(8,128)(2,1)}), bf16[1024,256]{0,1:T(8,128)(2,1)}) %reduce-scatter.5.cloned.1.call-update) | async-done | bytes 524304 | tf_op jit(solution)/shard_map/reduce_scatter | solution.py:102
  372.6 0.9 reshape_reshape.3
  373.5 111.3 %all-reduce.2.cloned.1.call-done = bf16[1024,256]{0,1:T(8,128)(2,1)} async-done(((bf16[1024,256]{0,1:T(8,128)(2,1)}), bf16[1024,256]{0,1:T(8,128)(2,1)}) %all-reduce.2.cloned.1.call-update) | async-done | bytes 524304 | tf_op jit(solution)/shard_map/psum | solution.py:110
  484.9 1.1 fusion.49
  486.0 1.0 copy.27
  487.0 1.0 copy.26
  (122 shorter events, 25.0 us)
Async XLA Ops:
  7.2 83.4 %all-gather.3.cloned.1.call-start = ((), (), s32[]{:S(2)}) async-start(), calls=%async_computation.2 | async-start | bytes 8912896 | tf_op jit(solution)/shard_map/all_gather | solution.py:77
  9.1 89.2 %copy-start.7 = (s32[1,8]{1,0:T(1,128)S(1)}, s32[1,8]{1,0:T(1,128)}, u32[]{:S(2)}) copy-start(s32[1,8]{1,0:T(1,128)} %param.15) | copy-start | bytes 100
  9.1 89.9 %copy-start.3 = (bf16[1,192,1024]{2,1,0:T(8,128)(2,1)S(1)}, bf16[1,192,1024]{2,1,0:T(8,128)(2,1)}, u32[]{:S(2)}) copy-start(bf16[1,192,1024]{2,1,0:T(8,128)(2,1)} %param.10) | copy-start | bytes 1179652
  9.1 128.6 %all-gather.5.cloned.1.call-start = ((), (), s32[]{:S(2)}) async-start(), calls=%async_computation.3 | async-start | bytes 1671168 | tf_op jit(solution)/shard_map/all_gather | solution.py:80
  98.2 2.9 copy-start.6
  98.3 174.9 %reduce-scatter.7.cloned.1.call-start = ((), (), s32[]{:S(2)}) async-start(), calls=%async_computation.6 | async-start | bytes 1671168
  140.3 1.9 copy-start.2
  140.3 1.9 copy-start.5
  143.0 1.1 copy-start
  145.2 1.1 copy-start.1
  149.7 1.9 copy-start.2
  149.7 1.9 copy-start.5
  152.4 1.1 copy-start
  154.6 1.1 copy-start.1
  159.1 1.9 copy-start.2
  159.1 1.9 copy-start.5
  161.8 1.1 copy-start
  164.0 1.1 copy-start.1
  168.5 1.9 copy-start.2
  168.5 1.9 copy-start.5
  171.2 1.1 copy-start
  173.4 1.1 copy-start.1
  177.9 1.9 copy-start.2
  177.9 1.9 copy-start.5
  180.6 1.1 copy-start
  182.8 1.1 copy-start.1
  187.3 1.9 copy-start.2
  187.3 1.9 copy-start.5
  190.0 1.1 copy-start
  192.2 1.1 copy-start.1
  196.7 1.9 copy-start.2
  196.7 1.9 copy-start.5
  199.4 1.1 copy-start
  201.6 1.1 copy-start.1
  206.1 1.9 copy-start.2
  206.1 1.9 copy-start.5
  208.8 1.1 copy-start
  211.0 1.1 copy-start.1
  219.5 152.8 %reduce-scatter.5.cloned.1.call-start = ((), (), s32[]{:S(2)}) async-start(), calls=%async_computation.4 | async-start | bytes 8912896 | tf_op jit(solution)/shard_map/reduce_scatter | solution.py:102
  281.6 90.7 %copy-start.4 = (bf16[8,192,128]{2,1,0:T(8,128)(2,1)S(1)}, bf16[8,192,128]{2,1,0:T(8,128)(2,1)}, u32[]{:S(2)}) copy-start(bf16[8,192,128]{2,1,0:T(8,128)(2,1)} %get-tuple-element.46) | copy-start | bytes 1179652
  281.6 203.2 %all-reduce.2.cloned.1.call-start = ((), (), s32[]{:S(2)}) async-start(), calls=%async_computation.5 | async-start | bytes 1048576 | tf_op jit(solution)/shard_map/psum | solution.py:110
Sparse Core Ops, SparseCore 0:
  11.0 79.5 all-gather.2
  98.4 39.2 all-gather.4
  219.6 53.5 reduce-scatter.6
  281.7 90.5 reduce-scatter.4
  374.6 110.2 all-reduce.1
where the time goes:
time: 496 us; the launch traced here: 495 us
  waiting for transfers between devices  370 us (75%)
  matrix products  61.1 us (12%)
  other arithmetic  28.8 us (6%)
  local copies, waits for them, and re-layouts  19.4 us (4%)
  between operations  13.9 us (3%)
    psum x1, waiting for transfers between devices, on_device(): weight_grads = lax.psum(partial_rows, 'ctx').astype(jnp.float32)  111 us
    reduce_scatter x1, waiting for transfers between devices, on_device(): lax.psum_scatter(lax.dot_general(columns, kv_grads, (((0,), (0,)), ((), (...  90.6 us
    all_gather x1, waiting for transfers between devices, on_device(): lax.all_gather(stacked, 'dp', axis=0, tiled=True)  81.4 us
    unnamed x6, waiting for transfers between devices  53.7 us
    all_gather x1, waiting for transfers between devices, on_device(): gathered = lax.all_gather(projected, 'ctx', axis=0, tiled=True)  33.1 us
    dot_general x8, matrix products, one_head(): jnp.dot(query_one, jnp.transpose(key_rows), preferred_element_type=jnp.fl...  15 us
  transfers between devices with their start and end apart: 5, of which 5 were waited for; matrix products, arithmetic and copies ran while one was open for 1% of the time, Pallas kernels for 0%

commit v1 on v0

v1 whole, which is shorter than its diff:
```python
import functools
import math

import jax
import jax.numpy as jnp
from jax import lax
from jax.experimental import pallas as pl
from jax.experimental.pallas import tpu as pltpu
from jax.sharding import PartitionSpec as P

MESH = pl.DeviceIdType.MESH
SIDE = 4
DEPTH = 8
BF = jnp.bfloat16
F32 = jnp.float32
VMEM_LIMIT = 60 * 2**20


def slot_of(x, y):
    return lax.rem(y, SIDE) * SIDE + lax.rem(x, SIDE)


class Place:
    def __init__(self):
        dp, ctx = lax.axis_index("dp"), lax.axis_index("ctx")
        self.dp, self.ctx = dp, ctx
        self.x, self.y = lax.rem(dp, SIDE), lax.div(dp, SIDE)
        self.z, self.core = lax.div(ctx, 2), lax.rem(ctx, 2)

    def partner(self):
        return (self.dp, self.z * 2 + 1 - self.core)

    def along_z(self, d):
        return (self.dp, lax.rem(self.z + d, DEPTH) * 2 + self.core)

    def along(self, axis, d):
        if axis == 0:
            return (slot_of(self.x + d, self.y), self.ctx)
        return (slot_of(self.x, self.y + d), self.ctx)

    def slot(self, half, du, dv):
        if half == 0:
            return slot_of(self.x + du, self.y + dv)
        return slot_of(self.x + dv, self.y + du)


def greet(devices):
    barrier = pltpu.get_barrier_semaphore()
    for device in devices:
        pl.semaphore_signal(barrier, inc=1, device_id=device, device_id_type=MESH)
    pl.semaphore_wait(barrier, len(devices))


class Sender:
    def __init__(self, sems):
        self.sems, self.sent = sems, []

    def __call__(self, src, dst, recv_sem, device):
        copy = pltpu.make_async_remote_copy(
            src_ref=src,
            dst_ref=dst,
            send_sem=self.sems.at[len(self.sent)],
            recv_sem=recv_sem,
            device_id=device,
            device_id_type=MESH,
        )
        copy.start()
        self.sent.append(copy)

    def finish(self):
        for copy in self.sent:
            copy.wait_send()


def arrived(dst, recv_sem, place):
    pltpu.make_async_remote_copy(
        src_ref=dst,
        dst_ref=dst,
        send_sem=recv_sem,
        recv_sem=recv_sem,
        device_id=place.partner(),
        device_id_type=MESH,
    ).wait_recv()


PROJECT_SENDS = 2 * 20 + 1 + 8 + 8


def project_kernel(
    hid_ref, wk_ref, wv_ref, kv_ref, hp_ref,
    hbuf, wbuf, acc, pin, pout,
    own_sem, hs_sem, hr_sem, hp_sem, s_sem, w_sem, p_sem, z_sem, c_sem,
):
    me = Place()
    rows, cols = hid_ref.shape[0], wbuf.shape[2]
    greet(
        [me.partner()]
        + [me.along(a, d) for a in (0, 1) for d in (1, SIDE - 1)]
        + [me.along_z(d) for d in (1, DEPTH - 1)]
    )
    send = Sender(s_sem)

    mine = pl.ds(pl.multiple_of(me.core * cols, cols), cols)
    wbuf[0, me.dp] = wk_ref[mine, :]
    wbuf[1, me.dp] = wv_ref[mine, :]
    half_rows = cols // 2
    parts = (pl.ds(0, half_rows), pl.ds(half_rows, half_rows))
    ahead, back = 1, SIDE - 1

    def w_send(h, slot, axis, d, part=None):
        ref = wbuf.at[h, slot]
        sem = w_sem.at[h, slot, 0 if part is None else part]
        if part is not None:
            ref = ref.at[parts[part]]
        send(ref, ref, sem, me.along(axis, d))

    def w_wait(h, slot, part=None):
        ref = wbuf.at[h, slot]
        if part is not None:
            ref = ref.at[parts[part]]
        arrived(ref, w_sem.at[h, slot, 0 if part is None else part], me)

    for d in (ahead, back):
        for h in (0, 1):
            w_send(h, me.dp, h, d)

    def part_of(s, core):
        return hid_ref.at[:, pl.ds(pl.multiple_of((s * 2 + core) * cols, cols), cols)]

    def h_copies(s):
        own = pltpu.make_async_copy(
            part_of(s, me.core), hbuf.at[s, pl.ds(0, rows)], own_sem.at[s]
        )
        other = pltpu.make_async_remote_copy(
            src_ref=part_of(s, 1 - me.core),
            dst_ref=hbuf.at[s, pl.ds(rows, rows)],
            send_sem=hs_sem.at[s],
            recv_sem=hr_sem.at[s],
            device_id=me.partner(),
            device_id_type=MESH,
        )
        keep = pltpu.make_async_copy(hbuf.at[s, pl.ds(rows, rows)], hp_ref.at[s], hp_sem.at[s])
        return own, other, keep

    @pl.loop(0, SIDE * SIDE)
    def _(i):
        s = slot_of(me.x + lax.rem(i, SIDE), me.y + lax.div(i, SIDE))
        own, other, _ = h_copies(s)
        own.start()
        other.start()

    for d in (ahead, back):
        for h in (0, 1):
            w_send(h, me.dp, 1 - h, d)

    acc[...] = jnp.zeros_like(acc)

    def compute(dx, dy):
        s = slot_of(me.x + dx, me.y + dy)
        own, other, keep = h_copies(s)
        own.wait()
        other.wait_recv()
        keep.start()
        w = jnp.concatenate([wbuf[0, s], wbuf[1, s]], axis=1)
        acc[...] += jnp.dot(hbuf[s], w, preferred_element_type=F32)

    for d, other, part in ((back, ahead, 0), (ahead, back, 1)):
        for h in (0, 1):
            slot = me.slot(h, d, 0)
            w_wait(h, slot)
            w_send(h, slot, h, other, part)
    for d in (back, ahead):
        for h in (0, 1):
            for e in (ahead, back):
                w_send(h, me.slot(h, d, 0), 1 - h, e)
    compute(0, 0)
    for h in (0, 1):
        slot = me.slot(h, 2, 0)
        w_wait(h, slot, 0)
        w_wait(h, slot, 1)
        for e in (ahead, back):
            w_send(h, slot, 1 - h, e)

    def pass_on(du):
        for d, other, part in ((back, ahead, 0), (ahead, back, 1)):
            for h in (0, 1):
                slot = me.slot(h, du, d)
                w_wait(h, slot)
                w_send(h, slot, 1 - h, other, part)

    pass_on(0)

    @pl.loop(0, 4)
    def _(i):
        a, b = lax.div(i, 2), lax.rem(i, 2)
        compute((1 - a) * (1 + 2 * b), a * (1 + 2 * b))

    pass_on(back)
    pass_on(ahead)

    @pl.loop(0, 4)
    def _(i):
        a, b = lax.div(i, 2), lax.rem(i, 2)
        compute(1 + 2 * a, 1 + 2 * b)

    pass_on(2)

    def far(du):
        for h in (0, 1):
            for part in (0, 1):
                w_wait(h, me.slot(h, du, 2), part)

    far(0)

    @pl.loop(0, 2)
    def _(i):
        compute(2 * i, 2 * (1 - i))

    far(back)
    far(ahead)

    @pl.loop(0, 4)
    def _(i):
        a, b = lax.div(i, 2), lax.rem(i, 2)
        compute((1 - a) * 2 + a * (1 + 2 * b), a * 2 + (1 - a) * (1 + 2 * b))

    far(2)
    compute(2, 2)

    pout[...] = acc[rows:, :]
    send(pout, pin, p_sem.at[0], me.partner())
    arrived(pin, p_sem.at[0], me)
    kv_ref[me.ctx] = (acc[:rows, :] + pin[...]).astype(BF)

    def block(d):
        return lax.rem(me.z + d, DEPTH) * 2 + me.core

    half = rows // 2
    z_parts = (pl.ds(0, half), pl.ds(half, half))

    def z_send(d, step, part=None):
        ref = kv_ref.at[block(d)]
        sem = z_sem.at[block(d), 0 if part is None else part]
        if part is not None:
            ref = ref.at[z_parts[part]]
        send(ref, ref, sem, me.along_z(step))

    def z_wait(d, part=None):
        ref = kv_ref.at[block(d)]
        sem = z_sem.at[block(d), 0 if part is None else part]
        if part is not None:
            ref = ref.at[z_parts[part]]
        arrived(ref, sem, me)

    def share(d):
        ref = kv_ref.at[block(d)]
        send(ref, ref, c_sem.at[block(d)], me.partner())

    up, down = 1, DEPTH - 1
    z_send(0, up)
    z_send(0, down)
    share(0)
    for k in (1, 2, 3):
        z_wait(DEPTH - k)
        z_send(DEPTH - k, up, 0 if k == 3 else None)
        z_wait(k)
        z_send(k, down, 1 if k == 3 else None)
        share(DEPTH - k)
        share(k)
    z_wait(4, 0)
    z_wait(4, 1)
    share(4)

    @pl.loop(0, DEPTH)
    def _(i):
        other = i * 2 + 1 - me.core
        arrived(kv_ref.at[other], c_sem.at[other], me)

    @pl.loop(0, SIDE * SIDE)
    def _(s):
        _, other, keep = h_copies(s)
        other.wait_send()
        keep.wait()

    send.finish()


def project(hidden, w_key, w_value):
    rows, width = hidden.shape
    n = SIDE * SIDE
    cols = width // n // 2
    hd = w_key.shape[1]
    dma = pltpu.SemaphoreType.DMA
    return pl.pallas_call(
        project_kernel,
        out_shape=(
            jax.ShapeDtypeStruct((2 * DEPTH, rows, 2 * hd), BF),
            jax.ShapeDtypeStruct((n, rows, cols), BF),
        ),
        in_specs=[pl.BlockSpec(memory_space=pl.ANY)] + [pl.BlockSpec(memory_space=pltpu.VMEM)] * 2,
        out_specs=(pl.BlockSpec(memory_space=pltpu.VMEM), pl.BlockSpec(memory_space=pl.ANY)),
        scratch_shapes=[
            pltpu.VMEM((n, 2 * rows, cols), BF),
            pltpu.VMEM((2, n, cols, hd), BF),
            pltpu.VMEM((2 * rows, 2 * hd), F32),
            pltpu.VMEM((rows, 2 * hd), F32),
            pltpu.VMEM((rows, 2 * hd), F32),
            dma((n,)),
            dma((n,)),
            dma((n,)),
            dma((n,)),
            dma((PROJECT_SENDS,)),
            dma((2, n, 2)),
            dma((1,)),
            dma((2 * DEPTH, 2)),
            dma((2 * DEPTH,)),
        ],
        compiler_params=pltpu.CompilerParams(
            collective_id=0, has_side_effects=True, vmem_limit_bytes=VMEM_LIMIT
        ),
        name="project",
    )(hidden, w_key, w_value)


STRETCH = 96
SPAN = 17
CHUNKS = 6


def attend_kernel(
    order_ref, lens_ref, ctx_ref, kv_ref, q_ref, g_ref, dq_ref, part_ref,
    kp, acc, qs, gs, scores, dprobs,
):
    heads, hd = q_ref.shape[1] // 128, 128
    n_stretch = kv_ref.shape[0] // STRETCH
    factor = math.log2(math.e) / math.sqrt(hd)
    scale = 1.0 / math.sqrt(hd)
    width = heads * STRETCH
    chunk = SPAN * STRETCH // CHUNKS

    @pl.loop(0, n_stretch)
    def _(b):
        src = pl.ds(pl.multiple_of(b * STRETCH, STRETCH), STRETCH)
        dst = pl.ds(pl.multiple_of(order_ref[b] * STRETCH, STRETCH), STRETCH)
        kp[dst, :] = kv_ref[src, :]
        acc[src, :] = jnp.zeros((STRETCH, 2 * hd), F32)

    for t in range(2):
        place = order_ref[ctx_ref[0] * 2 + t]
        first = jnp.maximum(place - (SPAN - 1), 0) * STRETCH
        for h in range(heads):
            at = (slice(t * STRETCH, (t + 1) * STRETCH), slice(h * hd, (h + 1) * hd))
            to = slice(h * STRETCH, (h + 1) * STRETCH)
            qs[to, :] = q_ref[at]
            gs[to, :] = g_ref[at]
        lane = lax.broadcasted_iota(jnp.int32, (1, width), 1)
        spot = place * STRETCH + lax.rem(lane, STRETCH)
        low = jnp.zeros_like(spot)
        end = jnp.int32(0)
        for d in range(lens_ref.shape[0]):
            end = end + lens_ref[d]
            low = jnp.where(spot >= end, end, low)

        def rows_of(c):
            return pl.ds(pl.multiple_of(first + c * chunk, 16), chunk)

        def local(c):
            return pl.ds(pl.multiple_of(c * chunk, 16), chunk)

        def score(c, top):
            k, v = kp[rows_of(c), :hd], kp[rows_of(c), hd:]
            nt = (((1,), (1,)), ((), ()))
            s = lax.dot_general(k, qs[...], nt, preferred_element_type=F32)
            at = first + c * chunk + lax.broadcasted_iota(jnp.int32, (chunk, width), 0)
            s = jnp.where((at >= low) & (at <= spot), s, -1e30)
            scores[local(c), :] = s
            dprobs[local(c), :] = lax.dot_general(v, gs[...], nt, preferred_element_type=F32)
            return jnp.maximum(top, jnp.max(s, axis=0, keepdims=True))

        top = lax.fori_loop(0, CHUNKS, score, jnp.full((1, width), -1e30, F32))

        def weigh(c, sums):
            total, mixed = sums
            e = jnp.exp2((scores[local(c), :] - top) * factor)
            scores[local(c), :] = e
            total = total + jnp.sum(e, axis=0, keepdims=True)
            mixed = mixed + jnp.sum(e * dprobs[local(c), :], axis=0, keepdims=True)
            return total, mixed

        zero = jnp.zeros((1, width), F32)
        total, mixed = lax.fori_loop(0, CHUNKS, weigh, (zero, zero))
        inverse = 1.0 / total
        delta = mixed * inverse

        def grads(c, dqt):
            p = scores[local(c), :] * inverse
            ds = (p * (dprobs[local(c), :] - delta)).astype(BF)
            k = kp[rows_of(c), :hd]
            acc[rows_of(c), :hd] += jnp.dot(ds, qs[...], preferred_element_type=F32)
            acc[rows_of(c), hd:] += jnp.dot(p.astype(BF), gs[...], preferred_element_type=F32)
            return dqt + lax.dot_general(
                k, ds, (((0,), (0,)), ((), ())), preferred_element_type=F32
            )

        dqt = lax.fori_loop(0, CHUNKS, grads, jnp.zeros((hd, width), F32))
        dq = (jnp.transpose(dqt) * scale).astype(BF)
        for h in range(heads):
            dq_ref[t * STRETCH : (t + 1) * STRETCH, h * hd : (h + 1) * hd] = dq[
                h * STRETCH : (h + 1) * STRETCH
            ]

    @pl.loop(0, n_stretch)
    def _(b):
        dst = pl.ds(pl.multiple_of(b * STRETCH, STRETCH), STRETCH)
        src = pl.ds(pl.multiple_of(order_ref[b] * STRETCH, STRETCH), STRETCH)
        part_ref[dst, :hd] = (acc[src, :hd] * scale).astype(BF)
        part_ref[dst, hd:] = acc[src, hd:].astype(BF)


def attend(order, lens, ctx, kv, queries, grad_out):
    seq, width = kv.shape
    span = SPAN * STRETCH
    heads = queries.shape[1] // 128
    smem = pl.BlockSpec(memory_space=pltpu.SMEM)
    vmem = pl.BlockSpec(memory_space=pltpu.VMEM)
    return pl.pallas_call(
        attend_kernel,
        out_shape=(
            jax.ShapeDtypeStruct(queries.shape, BF),
            jax.ShapeDtypeStruct(kv.shape, BF),
        ),
        in_specs=[smem] * 3 + [vmem] * 3,
        out_specs=(vmem, vmem),
        scratch_shapes=[
            pltpu.VMEM((seq, width), BF),
            pltpu.VMEM((seq, width), F32),
            pltpu.VMEM((heads * STRETCH, 128), BF),
            pltpu.VMEM((heads * STRETCH, 128), BF),
            pltpu.VMEM((span, heads * STRETCH), F32),
            pltpu.VMEM((span, heads * STRETCH), F32),
        ],
        compiler_params=pltpu.CompilerParams(vmem_limit_bytes=VMEM_LIMIT),
        name="attend",
    )(order, lens, ctx, kv, queries, grad_out)


WEIGHT_SENDS = 8 + 8 + 1 + 32 + 8 + 7 + 7 + 1


def weight_kernel(
    part_ref, hid_ref, hp_ref, out_ref,
    hbuf, tb, rbuf, zin, zout, gbuf, gt, pr0, pr1, qr0, qr1, fin, zr,
    own_sem, hp_sem, s_sem, d1_sem, d2_sem, d3_sem, p0_sem, p1_sem, q0_sem, q1_sem, f_sem, g_sem, c_sem,
):
    me = Place()
    rows, cols = gbuf.shape[1], hbuf.shape[2]
    n = SIDE * SIDE

    def h_copies(s):
        src = hid_ref.at[:, pl.ds(pl.multiple_of((s * 2 + me.core) * cols, cols), cols)]
        own = pltpu.make_async_copy(src, hbuf.at[s, pl.ds(0, rows)], own_sem.at[s])
        other = pltpu.make_async_copy(hp_ref.at[s], hbuf.at[s, pl.ds(rows, rows)], hp_sem.at[s])
        return own, other

    @pl.loop(0, n)
    def _(s):
        own, other = h_copies(s)
        own.start()
        other.start()

    greet(
        [me.partner()]
        + [me.along(a, d) for a in (0, 1) for d in (1, SIDE - 1)]
        + [me.along_z(d) for d in range(1, DEPTH)]
    )
    send = Sender(s_sem)

    for d in (4, 3, 5, 2, 6, 1, 7, 0):
        to = lax.rem(me.z + d, DEPTH)
        send(part_ref.at[to * 2 + 1 - me.core], rbuf.at[d], d1_sem.at[d], me.partner())

    def own_sum(d):
        arrived(rbuf.at[d], d1_sem.at[d], me)
        to = lax.rem(me.z + d, DEPTH)
        return part_ref[to * 2 + me.core].astype(F32) + rbuf[d].astype(F32)

    half = rows // 2
    z_parts = (pl.ds(0, half), pl.ds(half, half))
    steps = (1, DEPTH - 1)
    total = own_sum(4).astype(BF)
    for w in (0, 1):
        zout[w, 0, z_parts[w]] = total[w * half : (w + 1) * half]
        send(zout.at[w, 0, z_parts[w]], zin.at[w, 0, z_parts[w]], d2_sem.at[w, 0], me.along_z(steps[w]))
    for k in (1, 2, 3):
        for w in (0, 1):
            d = (4 - k) if w == 0 else DEPTH - (4 - k)
            total = own_sum(d)
            if k == 1:
                arrived(zin.at[w, 0, z_parts[w]], d2_sem.at[w, 0], me)
                zout[w, k] = total.astype(BF)
                got = zin[w, 0, z_parts[w]].astype(F32)
                zout[w, k, z_parts[w]] = (total[w * half : (w + 1) * half] + got).astype(BF)
            else:
                arrived(zin.at[w, k - 1], d2_sem.at[w, k - 1], me)
                zout[w, k] = (total + zin[w, k - 1].astype(F32)).astype(BF)
            send(zout.at[w, k], zin.at[w, k], d2_sem.at[w, k], me.along_z(steps[w]))
    total = own_sum(0)
    for w in (0, 1):
        arrived(zin.at[w, 3], d2_sem.at[w, 3], me)
        total = total + zin[w, 3].astype(F32)
    gbuf[0] = total.astype(BF)
    send(gbuf.at[0], gbuf.at[1], d3_sem.at[0], me.partner())
    gt[:, :rows] = jnp.transpose(total).astype(BF)

    @pl.loop(0, n)
    def _(s):
        own, other = h_copies(s)
        own.wait()
        other.wait()

    arrived(gbuf.at[1], d3_sem.at[0], me)
    gt[:, rows:] = jnp.transpose(gbuf[1].astype(F32)).astype(BF)

    def terms(dx, dy):
        s = slot_of(me.x + dx, me.y + dy)
        t = jnp.dot(gt[...], hbuf[s], preferred_element_type=F32).astype(BF)
        hd = t.shape[0] // 2
        tb[0, s] = t[:hd]
        tb[1, s] = t[hd:]

    hd = tb.shape[2]
    parts = (pl.ds(0, hd // 2), pl.ds(hd // 2, hd // 2))
    sides = (1, SIDE - 1)
    turn = (2, 1, 3, 0)

    def first_sends(h):
        for dv in turn:
            for w in (0, 1):
                send(tb.at[h, me.slot(h, 2, dv), parts[w]], pr0.at[h, w, dv], p0_sem.at[h, w, dv], me.along(h, sides[w]))

    @pl.loop(0, SIDE)
    def _(i):
        terms(2, i)

    first_sends(0)

    @pl.loop(0, SIDE - 1)
    def _(i):
        terms(i + lax.div(i, 2), 2)

    first_sends(1)

    @pl.loop(0, (SIDE - 1) * (SIDE - 1))
    def _(i):
        a, b = lax.div(i, 3), lax.rem(i, 3)
        terms(a + lax.div(a, 2), b + lax.div(b, 2))

    def add(h, slot, part, got):
        ref = tb.at[h, slot]
        if part is not None:
            ref = ref.at[parts[part]]
        ref[...] = (ref[...].astype(F32) + got.astype(F32)).astype(BF)

    for dv in turn:
        for h in (0, 1):
            for w in (0, 1):
                slot = me.slot(h, sides[w], dv)
                arrived(pr0.at[h, w, dv], p0_sem.at[h, w, dv], me)
                add(h, slot, w, pr0[h, w, dv])
                send(tb.at[h, slot], pr1.at[h, w, dv], p1_sem.at[h, w, dv], me.along(h, sides[w]))

    def collect(h, dv):
        for w in (0, 1):
            arrived(pr1.at[h, w, dv], p1_sem.at[h, w, dv], me)
        add(h, me.slot(h, 0, dv), None, pr1[h, 0, dv].astype(F32) + pr1[h, 1, dv].astype(F32))

    for h in (0, 1):
        collect(h, 2)
        for w in (0, 1):
            send(tb.at[h, me.slot(h, 0, 2), parts[w]], qr0.at[h, w], q0_sem.at[h, w], me.along(1 - h, sides[w]))
    for w in (0, 1):
        for h in (0, 1):
            slot = me.slot(h, 0, sides[w])
            collect(h, sides[w])
            arrived(qr0.at[h, w], q0_sem.at[h, w], me)
            add(h, slot, w, qr0[h, w])
            send(tb.at[h, slot], qr1.at[h, w], q1_sem.at[h, w], me.along(1 - h, sides[w]))
    for h in (0, 1):
        collect(h, 0)
        for w in (0, 1):
            arrived(qr1.at[h, w], q1_sem.at[h, w], me)
        got = qr1[h, 0].astype(F32) + qr1[h, 1].astype(F32)
        fin[h * hd : (h + 1) * hd] = (tb[h, me.dp].astype(F32) + got).astype(BF)

    piece = 2 * hd // DEPTH

    def eighth(d):
        return pl.ds(pl.multiple_of(lax.rem(me.z + d, DEPTH) * piece, piece), piece)

    for d in (4, 3, 5, 2, 6, 1, 7):
        send(fin.at[eighth(d)], zr.at[d], f_sem.at[d], me.along_z(d))
    total = fin[eighth(0)].astype(F32)
    for d in range(1, DEPTH):
        arrived(zr.at[d], f_sem.at[d], me)
        total = total + zr[d].astype(F32)
    out_ref[me.core, eighth(0)] = total.astype(BF)
    for d in (4, 3, 5, 2, 6, 1, 7):
        ref = out_ref.at[me.core, eighth(0)]
        send(ref, ref, g_sem.at[d], me.along_z(d))
    for d in range(1, DEPTH):
        arrived(out_ref.at[me.core, eighth(DEPTH - d)], g_sem.at[d], me)
    send(out_ref.at[me.core], out_ref.at[me.core], c_sem.at[0], me.partner())
    arrived(out_ref.at[1 - me.core], c_sem.at[0], me)
    send.finish()


def weight_grads(part, hidden, hidden_other):
    blocks, rows, width = part.shape
    n, _, cols = hidden_other.shape
    hd = width // 2
    dma = pltpu.SemaphoreType.DMA
    vmem, hbm = pl.BlockSpec(memory_space=pltpu.VMEM), pl.BlockSpec(memory_space=pl.ANY)
    return pl.pallas_call(
        weight_kernel,
        out_shape=jax.ShapeDtypeStruct((2, width, cols), BF),
        in_specs=[vmem, hbm, hbm],
        out_specs=vmem,
        scratch_shapes=[
            pltpu.VMEM((n, 2 * rows, cols), BF),
            pltpu.VMEM((2, n, hd, cols), BF),
            pltpu.VMEM((DEPTH, rows, width), BF),
            pltpu.VMEM((2, 4, rows, width), BF),
            pltpu.VMEM((2, 4, rows, width), BF),
            pltpu.VMEM((2, rows, width), BF),
            pltpu.VMEM((width, 2 * rows), BF),
            pltpu.VMEM((2, 2, SIDE, hd // 2, cols), BF),
            pltpu.VMEM((2, 2, SIDE, hd, cols), BF),
            pltpu.VMEM((2, 2, hd // 2, cols), BF),
            pltpu.VMEM((2, 2, hd, cols), BF),
            pltpu.VMEM((width, cols), BF),
            pltpu.VMEM((DEPTH, width // DEPTH, cols), BF),
            dma((n,)),
            dma((n,)),
            dma((WEIGHT_SENDS,)),
            dma((DEPTH,)),
            dma((2, 4)),
            dma((1,)),
            dma((2, 2, SIDE)),
            dma((2, 2, SIDE)),
            dma((2, 2)),
            dma((2, 2)),
            dma((DEPTH,)),
            dma((DEPTH,)),
            dma((1,)),
        ],
        compiler_params=pltpu.CompilerParams(
            collective_id=1, has_side_effects=True, vmem_limit_bytes=VMEM_LIMIT
        ),
        name="weights",
    )(part, hidden, hidden_other)


def on_device(hidden_in, queries, grad_out, w_key, w_value, stretch_order, doc_lengths):
    hidden = hidden_in[0]
    rows, hd = hidden.shape[0], w_key.shape[1]
    kv, hidden_other = project(hidden, w_key, w_value)
    ctx = lax.axis_index("ctx").astype(jnp.int32).reshape(1)
    query_grad, part = attend(
        stretch_order, doc_lengths[0], ctx, kv.reshape(-1, 2 * hd), queries[0], grad_out[0]
    )
    sums = weight_grads(part.reshape(kv.shape), hidden, hidden_other)

    def finish(t):
        return jnp.transpose(t, (0, 2, 1)).reshape(-1, hd).astype(F32)

    return query_grad[None], finish(sums[:, :hd]), finish(sums[:, hd:])


def solution(mesh):
    return jax.shard_map(
        on_device,
        mesh=mesh,
        in_specs=(
            P("dp", "ctx", None),
            P("dp", "ctx", None),
            P("dp", "ctx", None),
            P("dp", None),
            P("dp", None),
            P(),
            P("dp", None),
        ),
        out_specs=(P("dp", "ctx", None), P("dp", None), P("dp", None)),
        check_vma=False,
    )
```

time: 496 us -> 146 us (0.29)
  waiting for transfers between devices: 370 us -> 0 us
  Pallas kernels: 0 us -> 142 us
  matrix products: 61.1 us -> 0 us
  other arithmetic: 28.8 us -> 1.16 us
  local copies, waits for them, and re-layouts: 19.4 us -> 1.99 us
  between operations: 13.9 us -> 0.66 us
    pallas_call x0 -> x3, Pallas kernels: none -> 142 us  [the longest x1 68.9 us: weight_grads(): pl.pallas_call(weight_kernel, out_shape=jax.ShapeDtypeStruct((2, width, c...]
    all_gather x2 -> x0, waiting for transfers between devices: 114 us -> none  [the longest x1 81.4 us: on_device(): lax.all_gather(stacked, 'dp', axis=0, tiled=True)]
    psum x1 -> x0, waiting for transfers between devices: 111 us -> none  [on_device(): weight_grads = lax.psum(partial_rows, 'ctx').astype(jnp.float32)]
    reduce_scatter x1 -> x0, waiting for transfers between devices: 90.6 us -> none  [on_device(): lax.psum_scatter(lax.dot_general(columns, kv_grads, (((0,), (0,)), ((), (...]
    dot_general x50 -> x0, matrix products: 61.1 us -> none  [the longest x8 15 us: one_head(): jnp.dot(query_one, jnp.transpose(key_rows), preferred_element_type=jnp.fl...]
    unnamed x6 -> x0, waiting for transfers between devices: 53.7 us -> none
    reduce_sum x12 -> x0, other arithmetic: 9.63 us -> none  [the longest x8 6.18 us: one_head(): probabilities = expsum / jnp.sum(expsum, axis=-1, keepdims=True)]
    add x10 -> x0, other arithmetic: 8.5 us -> none  [the longest x8 8.47 us: one_head(): running + jnp.concatenate([key_grad, value_grad], axis=1)]
  transfers between devices with their start and end apart: 5 -> 0, of which waited for: 5 -> 0; matrix products, arithmetic and copies ran while one was open for 1% -> 0% of each run, Pallas kernels for 0% -> 0%
where the time goes in v1:
time: 146 us
  Pallas kernels  142 us (97%)
  local copies, waits for them, and re-layouts  1.99 us (1%)
    pallas_call x1, Pallas kernels, weight_grads(): pl.pallas_call(weight_kernel, out_shape=jax.ShapeDtypeStruct((2, width, c...  68.9 us
    pallas_call x1, Pallas kernels, project(): pl.pallas_call(project_kernel, out_shape=(jax.ShapeDtypeStruct((2 * DEPTH...  55.2 us
    pallas_call x1, Pallas kernels, attend(): pl.pallas_call(attend_kernel, out_shape=(jax.ShapeDtypeStruct(queries.sha...  17.8 us

profile of v1, /device:TPU:1, one launch (start us, length us, event | category | flops | bytes accessed | tf_op | source)
XLA Modules:
  0.0 145.7 jit_solution(15720085077538658550)
XLA Ops:
  0.6 55.2 %project.1 = (bf16[16,192,256]{2,1,0:T(8,128)(2,1)}, bf16[16,192,512]{2,1,0:T(8,128)(2,1)}) custom-call(bf16[192,16384]{1,0:T(8,128)(2,1)} %bitcast.14, bf16[1024,128]{1,0:T(8,128)(2,1)} %wk_ref.1, bf16[1024,128]{1,0:T(8,128)(2,1)} %wv_ref.1), custom_call_target="tpu_custom_call" | custom-call | tf_op jit(solution)/shard_map/project/pallas_call | solution.py:294
  55.8 17.8 %attend.1 = (bf16[192,1024]{1,0:T(8,128)(2,1)}, bf16[3072,256]{1,0:T(8,128)(2,1)}) custom-call(s32[32]{0:T(128)} %order_ref.1, s32[8]{0:T(128)} %bitcast.22, s32[1]{0:T(128)} %bitcast.1.ctx_ref, bf16[3072,256]{1,0:T(8,128)(2,1)} %bitcast.16, bf16[192,1024]{1,0:T(8,128)(2,1)} %bitcast.20, bf16[192,1024]{1,0:T(8,128)(2,1)} %bitcast.21), custom_call_target="tpu_custom_call" | custom-call | tf_op jit(solution)/shard_map/attend/pallas_call | solution.py:426
  73.6 68.9 %weights.1 = bf16[2,256,512]{2,1,0:T(8,128)(2,1)} custom-call(bf16[16,192,256]{2,1,0:T(8,128)(2,1)} %bitcast.17, bf16[192,16384]{1,0:T(8,128)(2,1)} %bitcast.15, bf16[16,192,512]{2,1,0:T(8,128)(2,1)} %get-tuple-element.10.hp_ref), custom_call_target="tpu_custom_call" | custom-call | tf_op jit(solution)/shard_map/weights/pallas_call | solution.py:623
  142.5 1.2 convert_bitcast_fusion
  143.7 1.0 copy.11
  144.7 1.0 copy.10

commit v2 on v1

--- a/solution.py
+++ b/solution.py
@@ -83,7 +83,7 @@
     ).wait_recv()
 
 
-PROJECT_SENDS = 2 * 20 + 1 + 8 + 8
+PROJECT_SENDS = 2 * 20 + 1 + 14 + 8
 
 
 def project_kernel(
@@ -238,33 +238,30 @@
     half = rows // 2
     z_parts = (pl.ds(0, half), pl.ds(half, half))
 
-    def z_send(d, step, part=None):
-        ref = kv_ref.at[block(d)]
-        sem = z_sem.at[block(d), 0 if part is None else part]
-        if part is not None:
-            ref = ref.at[z_parts[part]]
+    def z_send(d, step, part):
+        ref, sem = kv_ref.at[block(d), z_parts[part]], z_sem.at[block(d), part]
         send(ref, ref, sem, me.along_z(step))
 
-    def z_wait(d, part=None):
-        ref = kv_ref.at[block(d)]
-        sem = z_sem.at[block(d), 0 if part is None else part]
-        if part is not None:
-            ref = ref.at[z_parts[part]]
-        arrived(ref, sem, me)
+    def z_wait(d, part):
+        arrived(kv_ref.at[block(d), z_parts[part]], z_sem.at[block(d), part], me)
 
     def share(d):
         ref = kv_ref.at[block(d)]
         send(ref, ref, c_sem.at[block(d)], me.partner())
 
     up, down = 1, DEPTH - 1
-    z_send(0, up)
-    z_send(0, down)
+    for first in (0, 1):
+        z_send(0, up, first)
+        z_send(0, down, 1 - first)
     share(0)
     for k in (1, 2, 3):
-        z_wait(DEPTH - k)
-        z_send(DEPTH - k, up, 0 if k == 3 else None)
-        z_wait(k)
-        z_send(k, down, 1 if k == 3 else None)
+        for first in (0, 1):
+            z_wait(DEPTH - k, first)
+            if k < 3 or first == 0:
+                z_send(DEPTH - k, up, first)
+            z_wait(k, 1 - first)
+            if k < 3 or first == 0:
+                z_send(k, down, 1 - first)
         share(DEPTH - k)
         share(k)
     z_wait(4, 0)
@@ -324,7 +321,6 @@
 
 STRETCH = 96
 SPAN = 17
-CHUNKS = 6
 
 
 def attend_kernel(
@@ -336,7 +332,6 @@
     factor = math.log2(math.e) / math.sqrt(hd)
     scale = 1.0 / math.sqrt(hd)
     width = heads * STRETCH
-    chunk = SPAN * STRETCH // CHUNKS
 
     @pl.loop(0, n_stretch)
     def _(b):
@@ -361,48 +356,26 @@
             end = end + lens_ref[d]
             low = jnp.where(spot >= end, end, low)
 
-        def rows_of(c):
-            return pl.ds(pl.multiple_of(first + c * chunk, 16), chunk)
-
-        def local(c):
-            return pl.ds(pl.multiple_of(c * chunk, 16), chunk)
-
-        def score(c, top):
-            k, v = kp[rows_of(c), :hd], kp[rows_of(c), hd:]
-            nt = (((1,), (1,)), ((), ()))
-            s = lax.dot_general(k, qs[...], nt, preferred_element_type=F32)
-            at = first + c * chunk + lax.broadcasted_iota(jnp.int32, (chunk, width), 0)
-            s = jnp.where((at >= low) & (at <= spot), s, -1e30)
-            scores[local(c), :] = s
-            dprobs[local(c), :] = lax.dot_general(v, gs[...], nt, preferred_element_type=F32)
-            return jnp.maximum(top, jnp.max(s, axis=0, keepdims=True))
-
-        top = lax.fori_loop(0, CHUNKS, score, jnp.full((1, width), -1e30, F32))
-
-        def weigh(c, sums):
-            total, mixed = sums
-            e = jnp.exp2((scores[local(c), :] - top) * factor)
-            scores[local(c), :] = e
-            total = total + jnp.sum(e, axis=0, keepdims=True)
-            mixed = mixed + jnp.sum(e * dprobs[local(c), :], axis=0, keepdims=True)
-            return total, mixed
-
-        zero = jnp.zeros((1, width), F32)
-        total, mixed = lax.fori_loop(0, CHUNKS, weigh, (zero, zero))
-        inverse = 1.0 / total
-        delta = mixed * inverse
-
-        def grads(c, dqt):
-            p = scores[local(c), :] * inverse
-            ds = (p * (dprobs[local(c), :] - delta)).astype(BF)
-            k = kp[rows_of(c), :hd]
-            acc[rows_of(c), :hd] += jnp.dot(ds, qs[...], preferred_element_type=F32)
-            acc[rows_of(c), hd:] += jnp.dot(p.astype(BF), gs[...], preferred_element_type=F32)
-            return dqt + lax.dot_general(
-                k, ds, (((0,), (0,)), ((), ())), preferred_element_type=F32
-            )
-
-        dqt = lax.fori_loop(0, CHUNKS, grads, jnp.zeros((hd, width), F32))
+        window = pl.ds(pl.multiple_of(first, STRETCH), SPAN * STRETCH)
+        nt = (((1,), (1,)), ((), ()))
+        low, high = low - first, spot - first
+        at = lax.broadcasted_iota(jnp.int32, (SPAN * STRETCH, width), 0)
+        s = lax.dot_general(kp[window, :hd], qs[...], nt, preferred_element_type=F32)
+        s = jnp.where((at >= low) & (at <= high), s, -1e30)
+        scores[...] = s
+        top = jnp.max(s, axis=0, keepdims=True)
+        dprobs[...] = lax.dot_general(kp[window, hd:], gs[...], nt, preferred_element_type=F32)
+        e = jnp.exp2((scores[...] - top) * factor)
+        scores[...] = e
+        inverse = 1.0 / jnp.sum(e, axis=0, keepdims=True)
+        delta = jnp.sum(e * dprobs[...], axis=0, keepdims=True) * inverse
+        p = scores[...] * inverse
+        ds = (p * (dprobs[...] - delta)).astype(BF)
+        acc[window, :hd] += jnp.dot(ds, qs[...], preferred_element_type=F32)
+        acc[window, hd:] += jnp.dot(p.astype(BF), gs[...], preferred_element_type=F32)
+        dqt = lax.dot_general(
+            kp[window, :hd], ds, (((0,), (0,)), ((), ())), preferred_element_type=F32
+        )
         dq = (jnp.transpose(dqt) * scale).astype(BF)
         for h in range(heads):
             dq_ref[t * STRETCH : (t + 1) * STRETCH, h * hd : (h + 1) * hd] = dq[
@@ -444,13 +417,14 @@
     )(order, lens, ctx, kv, queries, grad_out)
 
 
-WEIGHT_SENDS = 8 + 8 + 1 + 32 + 8 + 7 + 7 + 1
+WEIGHT_SENDS = 8 + 14 + 2 + 32 + 8 + 14 + 7 + 15 + 7 + 8
+FLAT_ROWS = 80
 
 
 def weight_kernel(
     part_ref, hid_ref, hp_ref, out_ref,
-    hbuf, tb, rbuf, zin, zout, gbuf, gt, pr0, pr1, qr0, qr1, fin, zr,
-    own_sem, hp_sem, s_sem, d1_sem, d2_sem, d3_sem, p0_sem, p1_sem, q0_sem, q1_sem, f_sem, g_sem, c_sem,
+    hbuf, tb, rbuf, zin, zout, gbuf, gt, pr0, pr1, qr0, qr1, cin, zr, xr,
+    own_sem, hp_sem, s_sem, d1_sem, d2_sem, d3_sem, p0_sem, p1_sem, q0_sem, q1_sem, n_sem, f_sem, x_sem, g_sem, c_sem,
 ):
     me = Place()
     rows, cols = gbuf.shape[1], hbuf.shape[2]
@@ -471,46 +445,59 @@
     greet(
         [me.partner()]
         + [me.along(a, d) for a in (0, 1) for d in (1, SIDE - 1)]
-        + [me.along_z(d) for d in range(1, DEPTH)]
+        + [me.along_z(d) for d in (1, DEPTH - 1)]
     )
     send = Sender(s_sem)
+    z_steps = (1, DEPTH - 1)
+
+    def z_at(d):
+        return lax.rem(me.z + d, DEPTH)
+
+    def target(w, k):
+        return 4 - k if w == 0 else DEPTH - 4 + k
 
     for d in (4, 3, 5, 2, 6, 1, 7, 0):
-        to = lax.rem(me.z + d, DEPTH)
-        send(part_ref.at[to * 2 + 1 - me.core], rbuf.at[d], d1_sem.at[d], me.partner())
-
-    def own_sum(d):
-        arrived(rbuf.at[d], d1_sem.at[d], me)
-        to = lax.rem(me.z + d, DEPTH)
-        return part_ref[to * 2 + me.core].astype(F32) + rbuf[d].astype(F32)
+        send(part_ref.at[z_at(d) * 2 + 1 - me.core], rbuf.at[d], d1_sem.at[d], me.partner())
 
     half = rows // 2
-    z_parts = (pl.ds(0, half), pl.ds(half, half))
-    steps = (1, DEPTH - 1)
-    total = own_sum(4).astype(BF)
-    for w in (0, 1):
-        zout[w, 0, z_parts[w]] = total[w * half : (w + 1) * half]
-        send(zout.at[w, 0, z_parts[w]], zin.at[w, 0, z_parts[w]], d2_sem.at[w, 0], me.along_z(steps[w]))
+    pieces = (pl.ds(0, half), pl.ds(half, half))
+    known = set()
+
+    def own_sum(d, piece):
+        if d not in known:
+            known.add(d)
+            arrived(rbuf.at[d], d1_sem.at[d], me)
+        mine = part_ref[z_at(d) * 2 + me.core, pieces[piece]]
+        return mine.astype(F32) + rbuf[d, pieces[piece]].astype(F32)
+
+    def kv_step(w, k, piece, first):
+        total = own_sum(target(w, k), piece)
+        if not first:
+            arrived(zin.at[w, k - 1, pieces[piece]], d2_sem.at[w, k - 1, piece], me)
+            total = total + zin[w, k - 1, pieces[piece]].astype(F32)
+        ref = zout.at[w, k, pieces[piece]]
+        ref[...] = total.astype(BF)
+        send(ref, zin.at[w, k, pieces[piece]], d2_sem.at[w, k, piece], me.along_z(z_steps[w]))
+
+    for w in (0, 1):
+        kv_step(w, 0, w, True)
+    for w in (0, 1):
+        kv_step(w, 1, 1 - w, True)
     for k in (1, 2, 3):
         for w in (0, 1):
-            d = (4 - k) if w == 0 else DEPTH - (4 - k)
-            total = own_sum(d)
-            if k == 1:
-                arrived(zin.at[w, 0, z_parts[w]], d2_sem.at[w, 0], me)
-                zout[w, k] = total.astype(BF)
-                got = zin[w, 0, z_parts[w]].astype(F32)
-                zout[w, k, z_parts[w]] = (total[w * half : (w + 1) * half] + got).astype(BF)
-            else:
-                arrived(zin.at[w, k - 1], d2_sem.at[w, k - 1], me)
-                zout[w, k] = (total + zin[w, k - 1].astype(F32)).astype(BF)
-            send(zout.at[w, k], zin.at[w, k], d2_sem.at[w, k], me.along_z(steps[w]))
-    total = own_sum(0)
-    for w in (0, 1):
-        arrived(zin.at[w, 3], d2_sem.at[w, 3], me)
-        total = total + zin[w, 3].astype(F32)
-    gbuf[0] = total.astype(BF)
-    send(gbuf.at[0], gbuf.at[1], d3_sem.at[0], me.partner())
-    gt[:, :rows] = jnp.transpose(total).astype(BF)
+            kv_step(w, k, w, False)
+        if k < 3:
+            for w in (0, 1):
+                kv_step(w, k + 1, 1 - w, False)
+    for piece in (0, 1):
+        total = own_sum(0, piece)
+        for w in (0, 1):
+            arrived(zin.at[w, 3, pieces[piece]], d2_sem.at[w, 3, piece], me)
+            total = total + zin[w, 3, pieces[piece]].astype(F32)
+        ref = gbuf.at[0, pieces[piece]]
+        ref[...] = total.astype(BF)
+        send(ref, gbuf.at[1, pieces[piece]], d3_sem.at[piece], me.partner())
+    gt[:, :rows] = jnp.transpose(gbuf[0].astype(F32)).astype(BF)
 
     @pl.loop(0, n)
     def _(s):
@@ -518,25 +505,32 @@
         own.wait()
         other.wait()
 
-    arrived(gbuf.at[1], d3_sem.at[0], me)
+    for piece in (0, 1):
+        arrived(gbuf.at[1, pieces[piece]], d3_sem.at[piece], me)
     gt[:, rows:] = jnp.transpose(gbuf[1].astype(F32)).astype(BF)
+
+    hd = tb.shape[2]
+    groups = DEPTH // 2
 
     def terms(dx, dy):
         s = slot_of(me.x + dx, me.y + dy)
         t = jnp.dot(gt[...], hbuf[s], preferred_element_type=F32).astype(BF)
-        hd = t.shape[0] // 2
-        tb[0, s] = t[:hd]
-        tb[1, s] = t[hd:]
-
-    hd = tb.shape[2]
-    parts = (pl.ds(0, hd // 2), pl.ds(hd // 2, hd // 2))
+        for j in range(DEPTH):
+            h, g = divmod(j, groups)
+            tb[j, s] = t[h * hd : (h + 1) * hd, g * hd : (g + 1) * hd]
+
     sides = (1, SIDE - 1)
-    turn = (2, 1, 3, 0)
+
+    def flat(h, slot, dv, w=None):
+        cut = 48 if dv % 2 == 0 else 32
+        at = pl.ds(0, FLAT_ROWS) if w is None else pl.ds(0, cut) if w == 0 else pl.ds(cut, FLAT_ROWS - cut)
+        return tb.at[pl.ds(groups * h, groups), slot, at], at
 
     def first_sends(h):
-        for dv in turn:
+        for dv in (2, 1, 3, 0):
             for w in (0, 1):
-                send(tb.at[h, me.slot(h, 2, dv), parts[w]], pr0.at[h, w, dv], p0_sem.at[h, w, dv], me.along(h, sides[w]))
+                ref, at = flat(h, me.slot(h, 2, dv), dv, w)
+                send(ref, pr0.at[h, w, dv, :, at], p0_sem.at[h, w, dv], me.along(h, sides[w]))
 
     @pl.loop(0, SIDE)
     def _(i):
@@ -555,62 +549,124 @@
         a, b = lax.div(i, 3), lax.rem(i, 3)
         terms(a + lax.div(a, 2), b + lax.div(b, 2))
 
-    def add(h, slot, part, got):
-        ref = tb.at[h, slot]
-        if part is not None:
-            ref = ref.at[parts[part]]
-        ref[...] = (ref[...].astype(F32) + got.astype(F32)).astype(BF)
-
-    for dv in turn:
+    def add(ref, *got):
+        total = ref[...].astype(F32)
+        for g in got:
+            total = total + g.astype(F32)
+        ref[...] = total.astype(BF)
+
+    deep = pl.ds(FLAT_ROWS, hd - FLAT_ROWS)
+    slots = (pl.ds(0, n // 2), pl.ds(n // 2, n // 2))
+
+    def deep_step(k, w, piece, first=False):
+        ref = tb.at[z_at(target(w, k)), slots[piece], deep]
+        if not first:
+            got = cin.at[w, k - 1, slots[piece]]
+            arrived(got, n_sem.at[w, k - 1, piece], me)
+            add(ref, got[...])
+        send(ref, cin.at[w, k, slots[piece]], n_sem.at[w, k, piece], me.along_z(z_steps[w]))
+
+    def second_sends(dv):
         for h in (0, 1):
             for w in (0, 1):
                 slot = me.slot(h, sides[w], dv)
-                arrived(pr0.at[h, w, dv], p0_sem.at[h, w, dv], me)
-                add(h, slot, w, pr0[h, w, dv])
-                send(tb.at[h, slot], pr1.at[h, w, dv], p1_sem.at[h, w, dv], me.along(h, sides[w]))
+                ref, at = flat(h, slot, dv, w)
+                got = pr0.at[h, w, dv, :, at]
+                arrived(got, p0_sem.at[h, w, dv], me)
+                add(ref, got[...])
+                send(flat(h, slot, dv)[0], pr1.at[h, w, dv], p1_sem.at[h, w, dv], me.along(h, sides[w]))
 
     def collect(h, dv):
         for w in (0, 1):
             arrived(pr1.at[h, w, dv], p1_sem.at[h, w, dv], me)
-        add(h, me.slot(h, 0, dv), None, pr1[h, 0, dv].astype(F32) + pr1[h, 1, dv].astype(F32))
-
+        add(flat(h, me.slot(h, 0, dv), dv)[0], pr1[h, 0, dv], pr1[h, 1, dv])
+
+    def third_sends(h):
+        for w in (0, 1):
+            ref, at = flat(h, me.slot(h, 0, 2), h, w)
+            send(ref, qr0.at[h, w, :, at], q0_sem.at[h, w], me.along(1 - h, sides[w]))
+
+    def fourth_sends(h, w):
+        slot = me.slot(h, 0, sides[w])
+        ref, at = flat(h, slot, h, w)
+        got = qr0.at[h, w, :, at]
+        arrived(got, q0_sem.at[h, w], me)
+        add(ref, got[...])
+        send(flat(h, slot, 0)[0], qr1.at[h, w], q1_sem.at[h, w], me.along(1 - h, sides[w]))
+
+    for w in (0, 1):
+        deep_step(0, w, w, True)
+    for w in (0, 1):
+        deep_step(1, w, 1 - w, True)
+    second_sends(2)
+    second_sends(1)
+    for w in (0, 1):
+        deep_step(1, w, w)
+    second_sends(3)
+    second_sends(0)
+    for w in (0, 1):
+        deep_step(2, w, 1 - w)
     for h in (0, 1):
         collect(h, 2)
-        for w in (0, 1):
-            send(tb.at[h, me.slot(h, 0, 2), parts[w]], qr0.at[h, w], q0_sem.at[h, w], me.along(1 - h, sides[w]))
+        third_sends(h)
+    for w in (0, 1):
+        deep_step(2, w, w)
     for w in (0, 1):
         for h in (0, 1):
-            slot = me.slot(h, 0, sides[w])
             collect(h, sides[w])
-            arrived(qr0.at[h, w], q0_sem.at[h, w], me)
-            add(h, slot, w, qr0[h, w])
-            send(tb.at[h, slot], qr1.at[h, w], q1_sem.at[h, w], me.along(1 - h, sides[w]))
+            fourth_sends(h, w)
+    for w in (0, 1):
+        deep_step(3, w, 1 - w)
     for h in (0, 1):
         collect(h, 0)
+    for w in (0, 1):
+        deep_step(3, w, w)
+    for h in (0, 1):
         for w in (0, 1):
             arrived(qr1.at[h, w], q1_sem.at[h, w], me)
-        got = qr1[h, 0].astype(F32) + qr1[h, 1].astype(F32)
-        fin[h * hd : (h + 1) * hd] = (tb[h, me.dp].astype(F32) + got).astype(BF)
-
-    piece = 2 * hd // DEPTH
-
-    def eighth(d):
-        return pl.ds(pl.multiple_of(lax.rem(me.z + d, DEPTH) * piece, piece), piece)
-
+        add(flat(h, me.dp, 0)[0], qr1[h, 0], qr1[h, 1])
+    rows_first = pl.ds(0, FLAT_ROWS)
     for d in (4, 3, 5, 2, 6, 1, 7):
-        send(fin.at[eighth(d)], zr.at[d], f_sem.at[d], me.along_z(d))
-    total = fin[eighth(0)].astype(F32)
+        send(tb.at[z_at(d), me.dp, rows_first], zr.at[d], f_sem.at[d], me.along_z(d))
+    for piece in (0, 1):
+        ref = tb.at[me.z, slots[piece], deep]
+        for w in (0, 1):
+            arrived(cin.at[w, 3, slots[piece]], n_sem.at[w, 3, piece], me)
+        add(ref, cin[0, 3, slots[piece]], cin[1, 3, slots[piece]])
+    for far in range(4, 0, -1):
+        for dx in range(SIDE):
+            for dy in range(SIDE):
+                if min(dx, SIDE - dx) + min(dy, SIDE - dy) == far:
+                    slot = slot_of(me.x + dx, me.y + dy)
+                    send(tb.at[me.z, slot, deep], xr.at[dy * SIDE + dx], x_sem.at[dy * SIDE + dx], (slot, me.ctx))
+
+    top = tb[me.z, me.dp, rows_first].astype(F32)
     for d in range(1, DEPTH):
         arrived(zr.at[d], f_sem.at[d], me)
-        total = total + zr[d].astype(F32)
-    out_ref[me.core, eighth(0)] = total.astype(BF)
+        top = top + zr[d].astype(F32)
+    low = tb[me.z, me.dp, deep].astype(F32)
+    for i in range(1, n):
+        arrived(xr.at[i], x_sem.at[i], me)
+        low = low + xr[i].astype(F32)
+    done = jnp.transpose(jnp.concatenate([top, low], axis=0)).astype(BF)
+
+    def block(d, core):
+        j = z_at(d)
+        at = core * cols + lax.rem(j, groups) * hd
+        return out_ref.at[lax.div(j, groups), pl.ds(pl.multiple_of(at, hd), hd)]
+
+    def share(d):
+        send(block(d, me.core), block(d, me.core), c_sem.at[d], me.partner())
+
+    block(0, me.core)[...] = done
     for d in (4, 3, 5, 2, 6, 1, 7):
-        ref = out_ref.at[me.core, eighth(0)]
-        send(ref, ref, g_sem.at[d], me.along_z(d))
-    for d in range(1, DEPTH):
-        arrived(out_ref.at[me.core, eighth(DEPTH - d)], g_sem.at[d], me)
-    send(out_ref.at[me.core], out_ref.at[me.core], c_sem.at[0], me.partner())
-    arrived(out_ref.at[1 - me.core], c_sem.at[0], me)
+        send(block(0, me.core), block(0, me.core), g_sem.at[d], me.along_z(d))
+    share(0)
+    for d in (1, 7, 2, 6, 3, 5, 4):
+        arrived(block(d, me.core), g_sem.at[DEPTH - d], me)
+        share(d)
+    for d in range(DEPTH):
+        arrived(block(d, 1 - me.core), c_sem.at[d], me)
     send.finish()
 
 
@@ -619,39 +675,43 @@
     n, _, cols = hidden_other.shape
     hd = width // 2
     dma = pltpu.SemaphoreType.DMA
+    groups = DEPTH // 2
     vmem, hbm = pl.BlockSpec(memory_space=pltpu.VMEM), pl.BlockSpec(memory_space=pl.ANY)
     return pl.pallas_call(
         weight_kernel,
-        out_shape=jax.ShapeDtypeStruct((2, width, cols), BF),
+        out_shape=jax.ShapeDtypeStruct((2, 2 * cols, hd), BF),
         in_specs=[vmem, hbm, hbm],
         out_specs=vmem,
         scratch_shapes=[
             pltpu.VMEM((n, 2 * rows, cols), BF),
-            pltpu.VMEM((2, n, hd, cols), BF),
+            pltpu.VMEM((DEPTH, n, hd, hd), BF),
             pltpu.VMEM((DEPTH, rows, width), BF),
             pltpu.VMEM((2, 4, rows, width), BF),
             pltpu.VMEM((2, 4, rows, width), BF),
             pltpu.VMEM((2, rows, width), BF),
             pltpu.VMEM((width, 2 * rows), BF),
-            pltpu.VMEM((2, 2, SIDE, hd // 2, cols), BF),
-            pltpu.VMEM((2, 2, SIDE, hd, cols), BF),
-            pltpu.VMEM((2, 2, hd // 2, cols), BF),
-            pltpu.VMEM((2, 2, hd, cols), BF),
-            pltpu.VMEM((width, cols), BF),
-            pltpu.VMEM((DEPTH, width // DEPTH, cols), BF),
+            pltpu.VMEM((2, 2, SIDE, groups, FLAT_ROWS, hd), BF),
+            pltpu.VMEM((2, 2, SIDE, groups, FLAT_ROWS, hd), BF),
+            pltpu.VMEM((2, 2, groups, FLAT_ROWS, hd), BF),
+            pltpu.VMEM((2, 2, groups, FLAT_ROWS, hd), BF),
+            pltpu.VMEM((2, 4, n, hd - FLAT_ROWS, hd), BF),
+            pltpu.VMEM((DEPTH, FLAT_ROWS, hd), BF),
+            pltpu.VMEM((n, hd - FLAT_ROWS, hd), BF),
             dma((n,)),
             dma((n,)),
             dma((WEIGHT_SENDS,)),
             dma((DEPTH,)),
-            dma((2, 4)),
-            dma((1,)),
+            dma((2, 4, 2)),
+            dma((2,)),
             dma((2, 2, SIDE)),
             dma((2, 2, SIDE)),
             dma((2, 2)),
             dma((2, 2)),
+            dma((2, 4, 2)),
+            dma((DEPTH,)),
+            dma((n,)),
             dma((DEPTH,)),
             dma((DEPTH,)),
-            dma((1,)),
         ],
         compiler_params=pltpu.CompilerParams(
             collective_id=1, has_side_effects=True, vmem_limit_bytes=VMEM_LIMIT
@@ -670,10 +730,7 @@
     )
     sums = weight_grads(part.reshape(kv.shape), hidden, hidden_other)
 
-    def finish(t):
-        return jnp.transpose(t, (0, 2, 1)).reshape(-1, hd).astype(F32)
-
-    return query_grad[None], finish(sums[:, :hd]), finish(sums[:, hd:])
+    return query_grad[None], sums[0].astype(F32), sums[1].astype(F32)
 
 
 def solution(mesh):

time: 146 us -> 132 us (0.904)
  Pallas kernels: 142 us -> 129 us
  local copies, waits for them, and re-layouts: 1.99 us -> 0 us
    pallas_call x1, Pallas kernels: 68.9 us -> 61.5 us  [weight_grads(): pl.pallas_call(weight_kernel, out_shape=jax.ShapeDtypeStruct((2, 2 * cols...]
    pallas_call x1, Pallas kernels: 17.8 us -> 14.4 us  [attend(): pl.pallas_call(attend_kernel, out_shape=(jax.ShapeDtypeStruct(queries.sha...]
    pallas_call x1, Pallas kernels: 55.2 us -> 52.9 us  [project(): pl.pallas_call(project_kernel, out_shape=(jax.ShapeDtypeStruct((2 * DEPTH...]
    convert_element_type x2 -> x0, local copies, waits for them, and re-layouts: 1.99 us -> none  [finish(): return jnp.transpose(t, (0, 2, 1)).reshape(-1, hd).astype(F32)]
where the time goes in v2:
time: 132 us
  Pallas kernels  129 us (98%)
  other arithmetic  2.07 us (2%)
    pallas_call x1, Pallas kernels, weight_grads(): pl.pallas_call(weight_kernel, out_shape=jax.ShapeDtypeStruct((2, 2 * cols...  61.5 us
    pallas_call x1, Pallas kernels, project(): pl.pallas_call(project_kernel, out_shape=(jax.ShapeDtypeStruct((2 * DEPTH...  52.9 us
    pallas_call x1, Pallas kernels, attend(): pl.pallas_call(attend_kernel, out_shape=(jax.ShapeDtypeStruct(queries.sha...  14.4 us

profile of v2, /device:TPU:1, one launch (start us, length us, event | category | flops | bytes accessed | tf_op | source)
XLA Modules:
  0.0 131.5 jit_solution(8616331225958939823)
XLA Ops:
  0.6 52.9 %project.1 = (bf16[16,192,256]{2,1,0:T(8,128)(2,1)}, bf16[16,192,512]{2,1,0:T(8,128)(2,1)}) custom-call(bf16[192,16384]{1,0:T(8,128)(2,1)} %bitcast.14, bf16[1024,128]{1,0:T(8,128)(2,1)} %wk_ref.1, bf16[1024,128]{1,0:T(8,128)(2,1)} %wv_ref.1), custom_call_target="tpu_custom_call" | custom-call | tf_op jit(solution)/shard_map/project/pallas_call | solution.py:291
  53.5 14.4 %attend.1 = (bf16[192,1024]{1,0:T(8,128)(2,1)}, bf16[3072,256]{1,0:T(8,128)(2,1)}) custom-call(s32[32]{0:T(128)} %order_ref.1, s32[8]{0:T(128)} %bitcast.20, s32[1]{0:T(128)} %bitcast.1.ctx_ref, bf16[3072,256]{1,0:T(8,128)(2,1)} %bitcast.16, bf16[192,1024]{1,0:T(8,128)(2,1)} %bitcast.18, bf16[192,1024]{1,0:T(8,128)(2,1)} %bitcast.19), custom_call_target="tpu_custom_call" | custom-call | tf_op jit(solution)/shard_map/attend/pallas_call | solution.py:399
  67.9 61.5 %weights.1 = bf16[2,1024,128]{2,1,0:T(8,128)(2,1)} custom-call(bf16[16,192,256]{2,1,0:T(8,128)(2,1)} %bitcast.17, bf16[192,16384]{1,0:T(8,128)(2,1)} %bitcast.15, bf16[16,192,512]{2,1,0:T(8,128)(2,1)} %get-tuple-element.10.hp_ref), custom_call_target="tpu_custom_call" | custom-call | tf_op jit(solution)/shard_map/weights/pallas_call | solution.py:680
  129.5 2.1 %bitcast_convert_fusion = (f32[1024,128]{1,0:T(8,128)}, f32[1024,128]{1,0:T(8,128)}) fusion(bf16[2,1024,128]{2,1,0:T(8,128)(2,1)} %weights.1), kind=kLoop, calls=%fused_computation | loop fusion | flops 262144 | bytes 1572864 | tf_op jit(solution)/shard_map/convert_element_type | solution.py:733

commit v3 on v2

--- a/solution.py
+++ b/solution.py
@@ -1,4 +1,3 @@
-import functools
 import math
 
 import jax
@@ -14,6 +13,9 @@
 BF = jnp.bfloat16
 F32 = jnp.float32
 VMEM_LIMIT = 60 * 2**20
+STRETCH = 96
+SPAN = 17
+FLAT_ROWS = 80
 
 
 def slot_of(x, y):
@@ -48,7 +50,7 @@
     barrier = pltpu.get_barrier_semaphore()
     for device in devices:
         pl.semaphore_signal(barrier, inc=1, device_id=device, device_id_type=MESH)
-    pl.semaphore_wait(barrier, len(devices))
+    return lambda: pl.semaphore_wait(barrier, len(devices))
 
 
 class Sender:
@@ -83,54 +85,32 @@
     ).wait_recv()
 
 
-PROJECT_SENDS = 2 * 20 + 1 + 14 + 8
-
-
-def project_kernel(
-    hid_ref, wk_ref, wv_ref, kv_ref, hp_ref,
-    hbuf, wbuf, acc, pin, pout,
-    own_sem, hs_sem, hr_sem, hp_sem, s_sem, w_sem, p_sem, z_sem, c_sem,
+SENDS = 2 * 20 + 1 + 14 + 8 + 8 + 14 + 2 + 32 + 8 + 14 + 7 + 15 + 7 + 8
+
+
+def kernel(
+    hid_ref, q_ref, g_ref, wk_ref, wv_ref, order_ref, where_ref, lens_ref,
+    dq_ref, out_ref,
+    hbuf, wbuf, acc, pin, pout, kv_ref, qs, gs, kp, kw, scores, dprobs, sums, dqs,
+    tb, rout, rbuf, zin, zout, gbuf, gt, pr0, pr1, qr0, qr1, cin, zr, xr,
+    s_sem, own_sem, hs_sem, hr_sem, wo_sem, q_sem, go_sem, dq_sem, w_sem, p_sem, z_sem, c_sem,
+    d1_sem, d2_sem, d3_sem, p0_sem, p1_sem, q0_sem, q1_sem, n_sem, f_sem, x_sem, g_sem, b_sem,
 ):
+    heads = q_ref.shape[1] // wk_ref.shape[1]
     me = Place()
-    rows, cols = hid_ref.shape[0], wbuf.shape[2]
-    greet(
+    all_here = greet(
         [me.partner()]
         + [me.along(a, d) for a in (0, 1) for d in (1, SIDE - 1)]
         + [me.along_z(d) for d in (1, DEPTH - 1)]
     )
-    send = Sender(s_sem)
-
-    mine = pl.ds(pl.multiple_of(me.core * cols, cols), cols)
-    wbuf[0, me.dp] = wk_ref[mine, :]
-    wbuf[1, me.dp] = wv_ref[mine, :]
-    half_rows = cols // 2
-    parts = (pl.ds(0, half_rows), pl.ds(half_rows, half_rows))
-    ahead, back = 1, SIDE - 1
-
-    def w_send(h, slot, axis, d, part=None):
-        ref = wbuf.at[h, slot]
-        sem = w_sem.at[h, slot, 0 if part is None else part]
-        if part is not None:
-            ref = ref.at[parts[part]]
-        send(ref, ref, sem, me.along(axis, d))
-
-    def w_wait(h, slot, part=None):
-        ref = wbuf.at[h, slot]
-        if part is not None:
-            ref = ref.at[parts[part]]
-        arrived(ref, w_sem.at[h, slot, 0 if part is None else part], me)
-
-    for d in (ahead, back):
-        for h in (0, 1):
-            w_send(h, me.dp, h, d)
+    rows, cols, hd = hid_ref.shape[0], wbuf.shape[2], wbuf.shape[3]
+    n = SIDE * SIDE
 
     def part_of(s, core):
         return hid_ref.at[:, pl.ds(pl.multiple_of((s * 2 + core) * cols, cols), cols)]
 
     def h_copies(s):
-        own = pltpu.make_async_copy(
-            part_of(s, me.core), hbuf.at[s, pl.ds(0, rows)], own_sem.at[s]
-        )
+        own = pltpu.make_async_copy(part_of(s, me.core), hbuf.at[s, pl.ds(0, rows)], own_sem.at[s])
         other = pltpu.make_async_remote_copy(
             src_ref=part_of(s, 1 - me.core),
             dst_ref=hbuf.at[s, pl.ds(rows, rows)],
@@ -139,28 +119,68 @@
             device_id=me.partner(),
             device_id_type=MESH,
         )
-        keep = pltpu.make_async_copy(hbuf.at[s, pl.ds(rows, rows)], hp_ref.at[s], hp_sem.at[s])
-        return own, other, keep
-
-    @pl.loop(0, SIDE * SIDE)
-    def _(i):
-        s = slot_of(me.x + lax.rem(i, SIDE), me.y + lax.div(i, SIDE))
-        own, other, _ = h_copies(s)
-        own.start()
-        other.start()
+        return own, other
+
+    mine = pl.ds(pl.multiple_of(me.core * cols, cols), cols)
+    w_refs = (wk_ref.at[mine], wv_ref.at[mine])
+    w_own = [pltpu.make_async_copy(w_refs[h], wbuf.at[h, me.dp], wo_sem.at[h]) for h in (0, 1)]
+    for copy in w_own:
+        copy.start()
+
+    def q_copies(i):
+        t, h = lax.div(i, heads), lax.rem(i, heads)
+        src = (pl.ds(pl.multiple_of(t * STRETCH, STRETCH), STRETCH), pl.ds(pl.multiple_of(h * hd, hd), hd))
+        dst = pl.ds(pl.multiple_of(h * STRETCH, STRETCH), STRETCH)
+        return (
+            pltpu.make_async_copy(q_ref.at[src], qs.at[t, dst], q_sem.at[i]),
+            pltpu.make_async_copy(g_ref.at[src], gs.at[t, dst], go_sem.at[i]),
+        )
+
+    @pl.loop(0, n)
+    def _(i):
+        h_copies(slot_of(me.x + lax.rem(i, SIDE), me.y + lax.div(i, SIDE)))[0].start()
+
+    all_here()
+    send = Sender(s_sem)
+
+    half_rows = cols // 2
+    parts = (pl.ds(0, half_rows), pl.ds(half_rows, half_rows))
+    ahead, back = 1, SIDE - 1
+
+    def w_send(h, slot, axis, d, part=None):
+        ref = wbuf.at[h, slot]
+        sem = w_sem.at[h, slot, 0 if part is None else part]
+        if part is not None:
+            ref = ref.at[parts[part]]
+        send(ref, ref, sem, me.along(axis, d))
+
+    def w_wait(h, slot, part=None):
+        ref = wbuf.at[h, slot]
+        if part is not None:
+            ref = ref.at[parts[part]]
+        arrived(ref, w_sem.at[h, slot, 0 if part is None else part], me)
 
     for d in (ahead, back):
         for h in (0, 1):
-            w_send(h, me.dp, 1 - h, d)
+            send(w_refs[h], wbuf.at[h, me.dp], w_sem.at[h, me.dp, 0], me.along(h, d))
+
+    for d in (ahead, back):
+        for h in (0, 1):
+            send(w_refs[h], wbuf.at[h, me.dp], w_sem.at[h, me.dp, 0], me.along(1 - h, d))
+
+    @pl.loop(0, n)
+    def _(i):
+        h_copies(slot_of(me.x + lax.rem(i, SIDE), me.y + lax.div(i, SIDE)))[1].start()
 
     acc[...] = jnp.zeros_like(acc)
+    for copy in w_own:
+        copy.wait()
 
     def compute(dx, dy):
         s = slot_of(me.x + dx, me.y + dy)
-        own, other, keep = h_copies(s)
+        own, other = h_copies(s)
         own.wait()
         other.wait_recv()
-        keep.start()
         w = jnp.concatenate([wbuf[0, s], wbuf[1, s]], axis=1)
         acc[...] += jnp.dot(hbuf[s], w, preferred_element_type=F32)
 
@@ -227,26 +247,37 @@
     far(2)
     compute(2, 2)
 
+    def kv_block(ctx):
+        return pl.ds(ctx * 2, 2)
+
     pout[...] = acc[rows:, :]
     send(pout, pin, p_sem.at[0], me.partner())
+
+    @pl.loop(0, 2 * heads)
+    def _(i):
+        for copy in q_copies(i):
+            copy.start()
+
     arrived(pin, p_sem.at[0], me)
-    kv_ref[me.ctx] = (acc[:rows, :] + pin[...]).astype(BF)
+    kv_ref[kv_block(me.ctx)] = (acc[:rows, :] + pin[...]).astype(BF).reshape(2, STRETCH, 2 * hd)
 
     def block(d):
         return lax.rem(me.z + d, DEPTH) * 2 + me.core
 
     half = rows // 2
-    z_parts = (pl.ds(0, half), pl.ds(half, half))
+
+    def z_part(d, part):
+        return kv_ref.at[block(d) * 2 + part]
 
     def z_send(d, step, part):
-        ref, sem = kv_ref.at[block(d), z_parts[part]], z_sem.at[block(d), part]
+        ref, sem = z_part(d, part), z_sem.at[block(d), part]
         send(ref, ref, sem, me.along_z(step))
 
     def z_wait(d, part):
-        arrived(kv_ref.at[block(d), z_parts[part]], z_sem.at[block(d), part], me)
+        arrived(z_part(d, part), z_sem.at[block(d), part], me)
 
     def share(d):
-        ref = kv_ref.at[block(d)]
+        ref = kv_ref.at[kv_block(block(d))]
         send(ref, ref, c_sem.at[block(d)], me.partner())
 
     up, down = 1, DEPTH - 1
@@ -254,6 +285,7 @@
         z_send(0, up, first)
         z_send(0, down, 1 - first)
     share(0)
+
     for k in (1, 2, 3):
         for first in (0, 1):
             z_wait(DEPTH - k, first)
@@ -271,183 +303,76 @@
     @pl.loop(0, DEPTH)
     def _(i):
         other = i * 2 + 1 - me.core
-        arrived(kv_ref.at[other], c_sem.at[other], me)
-
-    @pl.loop(0, SIDE * SIDE)
-    def _(s):
-        _, other, keep = h_copies(s)
-        other.wait_send()
-        keep.wait()
-
-    send.finish()
-
-
-def project(hidden, w_key, w_value):
-    rows, width = hidden.shape
-    n = SIDE * SIDE
-    cols = width // n // 2
-    hd = w_key.shape[1]
-    dma = pltpu.SemaphoreType.DMA
-    return pl.pallas_call(
-        project_kernel,
-        out_shape=(
-            jax.ShapeDtypeStruct((2 * DEPTH, rows, 2 * hd), BF),
-            jax.ShapeDtypeStruct((n, rows, cols), BF),
-        ),
-        in_specs=[pl.BlockSpec(memory_space=pl.ANY)] + [pl.BlockSpec(memory_space=pltpu.VMEM)] * 2,
-        out_specs=(pl.BlockSpec(memory_space=pltpu.VMEM), pl.BlockSpec(memory_space=pl.ANY)),
-        scratch_shapes=[
-            pltpu.VMEM((n, 2 * rows, cols), BF),
-            pltpu.VMEM((2, n, cols, hd), BF),
-            pltpu.VMEM((2 * rows, 2 * hd), F32),
-            pltpu.VMEM((rows, 2 * hd), F32),
-            pltpu.VMEM((rows, 2 * hd), F32),
-            dma((n,)),
-            dma((n,)),
-            dma((n,)),
-            dma((n,)),
-            dma((PROJECT_SENDS,)),
-            dma((2, n, 2)),
-            dma((1,)),
-            dma((2 * DEPTH, 2)),
-            dma((2 * DEPTH,)),
-        ],
-        compiler_params=pltpu.CompilerParams(
-            collective_id=0, has_side_effects=True, vmem_limit_bytes=VMEM_LIMIT
-        ),
-        name="project",
-    )(hidden, w_key, w_value)
-
-
-STRETCH = 96
-SPAN = 17
-
-
-def attend_kernel(
-    order_ref, lens_ref, ctx_ref, kv_ref, q_ref, g_ref, dq_ref, part_ref,
-    kp, acc, qs, gs, scores, dprobs,
-):
-    heads, hd = q_ref.shape[1] // 128, 128
-    n_stretch = kv_ref.shape[0] // STRETCH
+        arrived(kv_ref.at[kv_block(other)], c_sem.at[other], me)
+
+
     factor = math.log2(math.e) / math.sqrt(hd)
     scale = 1.0 / math.sqrt(hd)
     width = heads * STRETCH
-
-    @pl.loop(0, n_stretch)
-    def _(b):
-        src = pl.ds(pl.multiple_of(b * STRETCH, STRETCH), STRETCH)
-        dst = pl.ds(pl.multiple_of(order_ref[b] * STRETCH, STRETCH), STRETCH)
-        kp[dst, :] = kv_ref[src, :]
-        acc[src, :] = jnp.zeros((STRETCH, 2 * hd), F32)
-
-    for t in range(2):
-        place = order_ref[ctx_ref[0] * 2 + t]
-        first = jnp.maximum(place - (SPAN - 1), 0) * STRETCH
-        for h in range(heads):
-            at = (slice(t * STRETCH, (t + 1) * STRETCH), slice(h * hd, (h + 1) * hd))
-            to = slice(h * STRETCH, (h + 1) * STRETCH)
-            qs[to, :] = q_ref[at]
-            gs[to, :] = g_ref[at]
-        lane = lax.broadcasted_iota(jnp.int32, (1, width), 1)
-        spot = place * STRETCH + lax.rem(lane, STRETCH)
+    nt = (((1,), (1,)), ((), ()))
+
+    def first_of(t):
+        return jnp.maximum(order_ref[me.ctx * 2 + t] - (SPAN - 1), 0)
+
+    @pl.loop(0, 2 * heads)
+    def _(i):
+        for copy in q_copies(i):
+            copy.wait()
+
+    @pl.loop(0, where_ref.shape[0])
+    def _(i):
+        kp[i] = kv_ref[where_ref[i]]
+
+    for t in (0, 1):
+        for at in (0, SPAN + 1):
+            sums[t, at] = jnp.zeros((STRETCH, 2 * hd), F32)
+    inner = slice(1, SPAN + 1)
+
+    @pl.loop(0, 2)
+    def _(t):
+        place, first = order_ref[me.ctx * 2 + t], first_of(t)
+
+        @pl.loop(0, SPAN)
+        def _(i):
+            kw[pl.ds(pl.multiple_of(i * STRETCH, STRETCH), STRETCH)] = kp[first + i]
+
+        spot = place * STRETCH + lax.rem(lax.broadcasted_iota(jnp.int32, (1, width), 1), STRETCH)
         low = jnp.zeros_like(spot)
         end = jnp.int32(0)
         for d in range(lens_ref.shape[0]):
             end = end + lens_ref[d]
             low = jnp.where(spot >= end, end, low)
-
-        window = pl.ds(pl.multiple_of(first, STRETCH), SPAN * STRETCH)
-        nt = (((1,), (1,)), ((), ()))
-        low, high = low - first, spot - first
+        low, high = low - first * STRETCH, spot - first * STRETCH
         at = lax.broadcasted_iota(jnp.int32, (SPAN * STRETCH, width), 0)
-        s = lax.dot_general(kp[window, :hd], qs[...], nt, preferred_element_type=F32)
+        s = lax.dot_general(kw[:, :hd], qs[t], nt, preferred_element_type=F32)
         s = jnp.where((at >= low) & (at <= high), s, -1e30)
         scores[...] = s
         top = jnp.max(s, axis=0, keepdims=True)
-        dprobs[...] = lax.dot_general(kp[window, hd:], gs[...], nt, preferred_element_type=F32)
+        dprobs[...] = lax.dot_general(kw[:, hd:], gs[t], nt, preferred_element_type=F32)
         e = jnp.exp2((scores[...] - top) * factor)
         scores[...] = e
         inverse = 1.0 / jnp.sum(e, axis=0, keepdims=True)
         delta = jnp.sum(e * dprobs[...], axis=0, keepdims=True) * inverse
         p = scores[...] * inverse
         ds = (p * (dprobs[...] - delta)).astype(BF)
-        acc[window, :hd] += jnp.dot(ds, qs[...], preferred_element_type=F32)
-        acc[window, hd:] += jnp.dot(p.astype(BF), gs[...], preferred_element_type=F32)
-        dqt = lax.dot_general(
-            kp[window, :hd], ds, (((0,), (0,)), ((), ())), preferred_element_type=F32
-        )
+        sums[t, inner, :, :hd] = jnp.dot(ds, qs[t], preferred_element_type=F32).reshape(SPAN, STRETCH, hd)
+        sums[t, inner, :, hd:] = jnp.dot(p.astype(BF), gs[t], preferred_element_type=F32).reshape(SPAN, STRETCH, hd)
+        dqt = lax.dot_general(kw[:, :hd], ds, (((0,), (0,)), ((), ())), preferred_element_type=F32)
         dq = (jnp.transpose(dqt) * scale).astype(BF)
+        row = pl.ds(pl.multiple_of(t * STRETCH, STRETCH), STRETCH)
         for h in range(heads):
-            dq_ref[t * STRETCH : (t + 1) * STRETCH, h * hd : (h + 1) * hd] = dq[
-                h * STRETCH : (h + 1) * STRETCH
-            ]
-
-    @pl.loop(0, n_stretch)
-    def _(b):
-        dst = pl.ds(pl.multiple_of(b * STRETCH, STRETCH), STRETCH)
-        src = pl.ds(pl.multiple_of(order_ref[b] * STRETCH, STRETCH), STRETCH)
-        part_ref[dst, :hd] = (acc[src, :hd] * scale).astype(BF)
-        part_ref[dst, hd:] = acc[src, hd:].astype(BF)
-
-
-def attend(order, lens, ctx, kv, queries, grad_out):
-    seq, width = kv.shape
-    span = SPAN * STRETCH
-    heads = queries.shape[1] // 128
-    smem = pl.BlockSpec(memory_space=pltpu.SMEM)
-    vmem = pl.BlockSpec(memory_space=pltpu.VMEM)
-    return pl.pallas_call(
-        attend_kernel,
-        out_shape=(
-            jax.ShapeDtypeStruct(queries.shape, BF),
-            jax.ShapeDtypeStruct(kv.shape, BF),
-        ),
-        in_specs=[smem] * 3 + [vmem] * 3,
-        out_specs=(vmem, vmem),
-        scratch_shapes=[
-            pltpu.VMEM((seq, width), BF),
-            pltpu.VMEM((seq, width), F32),
-            pltpu.VMEM((heads * STRETCH, 128), BF),
-            pltpu.VMEM((heads * STRETCH, 128), BF),
-            pltpu.VMEM((span, heads * STRETCH), F32),
-            pltpu.VMEM((span, heads * STRETCH), F32),
-        ],
-        compiler_params=pltpu.CompilerParams(vmem_limit_bytes=VMEM_LIMIT),
-        name="attend",
-    )(order, lens, ctx, kv, queries, grad_out)
-
-
-WEIGHT_SENDS = 8 + 14 + 2 + 32 + 8 + 14 + 7 + 15 + 7 + 8
-FLAT_ROWS = 80
-
-
-def weight_kernel(
-    part_ref, hid_ref, hp_ref, out_ref,
-    hbuf, tb, rbuf, zin, zout, gbuf, gt, pr0, pr1, qr0, qr1, cin, zr, xr,
-    own_sem, hp_sem, s_sem, d1_sem, d2_sem, d3_sem, p0_sem, p1_sem, q0_sem, q1_sem, n_sem, f_sem, x_sem, g_sem, c_sem,
-):
-    me = Place()
-    rows, cols = gbuf.shape[1], hbuf.shape[2]
-    n = SIDE * SIDE
-
-    def h_copies(s):
-        src = hid_ref.at[:, pl.ds(pl.multiple_of((s * 2 + me.core) * cols, cols), cols)]
-        own = pltpu.make_async_copy(src, hbuf.at[s, pl.ds(0, rows)], own_sem.at[s])
-        other = pltpu.make_async_copy(hp_ref.at[s], hbuf.at[s, pl.ds(rows, rows)], hp_sem.at[s])
-        return own, other
-
-    @pl.loop(0, n)
-    def _(s):
-        own, other = h_copies(s)
-        own.start()
-        other.start()
-
-    greet(
-        [me.partner()]
-        + [me.along(a, d) for a in (0, 1) for d in (1, SIDE - 1)]
-        + [me.along_z(d) for d in (1, DEPTH - 1)]
-    )
-    send = Sender(s_sem)
+            dqs[row, h * hd : (h + 1) * hd] = dq[h * STRETCH : (h + 1) * STRETCH]
+
+    dq_copy = pltpu.make_async_copy(dqs, dq_ref, dq_sem.at[0])
+    dq_copy.start()
+
+    def stretch_grads(b):
+        total = jnp.zeros((STRETCH, 2 * hd), F32)
+        for t in (0, 1):
+            i = jnp.minimum(jnp.maximum(order_ref[b] - first_of(t) + 1, 0), SPAN + 1)
+            total = total + sums[t, i]
+        return jnp.concatenate([total[:, :hd] * scale, total[:, hd:]], axis=1)
+
     z_steps = (1, DEPTH - 1)
 
     def z_at(d):
@@ -456,19 +381,23 @@
     def target(w, k):
         return 4 - k if w == 0 else DEPTH - 4 + k
 
+    pieces = (pl.ds(0, STRETCH), pl.ds(STRETCH, STRETCH))
+
+    def stretch(d, core, piece):
+        return (z_at(d) * 2 + core) * 2 + piece
+
     for d in (4, 3, 5, 2, 6, 1, 7, 0):
-        send(part_ref.at[z_at(d) * 2 + 1 - me.core], rbuf.at[d], d1_sem.at[d], me.partner())
-
-    half = rows // 2
-    pieces = (pl.ds(0, half), pl.ds(half, half))
+        for piece in (0, 1):
+            rout[d, pieces[piece]] = stretch_grads(stretch(d, 1 - me.core, piece)).astype(BF)
+        send(rout.at[d], rbuf.at[d], d1_sem.at[d], me.partner())
+
     known = set()
 
     def own_sum(d, piece):
         if d not in known:
             known.add(d)
             arrived(rbuf.at[d], d1_sem.at[d], me)
-        mine = part_ref[z_at(d) * 2 + me.core, pieces[piece]]
-        return mine.astype(F32) + rbuf[d, pieces[piece]].astype(F32)
+        return stretch_grads(stretch(d, me.core, piece)) + rbuf[d, pieces[piece]].astype(F32)
 
     def kv_step(w, k, piece, first):
         total = own_sum(target(w, k), piece)
@@ -499,17 +428,10 @@
         send(ref, gbuf.at[1, pieces[piece]], d3_sem.at[piece], me.partner())
     gt[:, :rows] = jnp.transpose(gbuf[0].astype(F32)).astype(BF)
 
-    @pl.loop(0, n)
-    def _(s):
-        own, other = h_copies(s)
-        own.wait()
-        other.wait()
-
     for piece in (0, 1):
         arrived(gbuf.at[1, pieces[piece]], d3_sem.at[piece], me)
     gt[:, rows:] = jnp.transpose(gbuf[1].astype(F32)).astype(BF)
 
-    hd = tb.shape[2]
     groups = DEPTH // 2
 
     def terms(dx, dy):
@@ -655,36 +577,88 @@
         at = core * cols + lax.rem(j, groups) * hd
         return out_ref.at[lax.div(j, groups), pl.ds(pl.multiple_of(at, hd), hd)]
 
-    def share(d):
-        send(block(d, me.core), block(d, me.core), c_sem.at[d], me.partner())
+    def share_block(d):
+        send(block(d, me.core), block(d, me.core), b_sem.at[d], me.partner())
 
     block(0, me.core)[...] = done
     for d in (4, 3, 5, 2, 6, 1, 7):
         send(block(0, me.core), block(0, me.core), g_sem.at[d], me.along_z(d))
-    share(0)
+    share_block(0)
     for d in (1, 7, 2, 6, 3, 5, 4):
         arrived(block(d, me.core), g_sem.at[DEPTH - d], me)
-        share(d)
+        share_block(d)
     for d in range(DEPTH):
-        arrived(block(d, 1 - me.core), c_sem.at[d], me)
+        arrived(block(d, 1 - me.core), b_sem.at[d], me)
     send.finish()
-
-
-def weight_grads(part, hidden, hidden_other):
-    blocks, rows, width = part.shape
-    n, _, cols = hidden_other.shape
-    hd = width // 2
+    dq_copy.wait()
+
+    @pl.loop(0, n)
+    def _(s):
+        h_copies(s)[1].wait_send()
+
+
+def finish_kernel(dq_ref, sums_ref, dq_out, key_out, value_out):
+    dq_out[...] = dq_ref[...]
+    key_out[...] = sums_ref[0].astype(F32)
+    value_out[...] = sums_ref[1].astype(F32)
+
+
+def finish(query_grad, sums):
+    steps = 4
+    (rows, width), (_, depth, hd) = query_grad.shape, sums.shape
+    dq_spec = pl.BlockSpec((rows // steps, width), lambda i: (i, 0))
+    out_spec = pl.BlockSpec((depth // steps, hd), lambda i: (i, 0))
+    return pl.pallas_call(
+        finish_kernel,
+        grid=(steps,),
+        out_shape=(
+            jax.ShapeDtypeStruct(query_grad.shape, BF),
+            jax.ShapeDtypeStruct((depth, hd), F32),
+            jax.ShapeDtypeStruct((depth, hd), F32),
+        ),
+        in_specs=[dq_spec, pl.BlockSpec((2, depth // steps, hd), lambda i: (0, i, 0))],
+        out_specs=(dq_spec, out_spec, out_spec),
+        name="finish",
+    )(query_grad, sums)
+
+
+def on_device(hidden_in, queries, grad_out, w_key, w_value, stretch_order, doc_lengths):
+    hidden = hidden_in[0]
+    rows, hd = hidden.shape[0], w_key.shape[1]
+    n = SIDE * SIDE
+    cols = hidden.shape[1] // n // 2
+    width, span = 2 * hd, SPAN * STRETCH
+    heads = queries.shape[2] // hd
+    groups = DEPTH // 2
+    every = jnp.arange(stretch_order.shape[0], dtype=jnp.int32)
+    stored_at = jnp.sum(jnp.where(stretch_order[None, :] == every[:, None], every[None, :], 0), axis=1)
     dma = pltpu.SemaphoreType.DMA
-    groups = DEPTH // 2
-    vmem, hbm = pl.BlockSpec(memory_space=pltpu.VMEM), pl.BlockSpec(memory_space=pl.ANY)
-    return pl.pallas_call(
-        weight_kernel,
-        out_shape=jax.ShapeDtypeStruct((2, 2 * cols, hd), BF),
-        in_specs=[vmem, hbm, hbm],
-        out_specs=vmem,
+    smem, hbm = pl.BlockSpec(memory_space=pltpu.SMEM), pl.BlockSpec(memory_space=pl.ANY)
+    query_grad, sums = pl.pallas_call(
+        kernel,
+        out_shape=(
+            jax.ShapeDtypeStruct((rows, heads * hd), BF),
+            jax.ShapeDtypeStruct((2, 2 * cols, hd), BF),
+        ),
+        in_specs=[hbm] * 5 + [smem] * 3,
+        out_specs=(hbm, pl.BlockSpec(memory_space=pltpu.VMEM)),
         scratch_shapes=[
             pltpu.VMEM((n, 2 * rows, cols), BF),
+            pltpu.VMEM((2, n, cols, hd), BF),
+            pltpu.VMEM((2 * rows, width), F32),
+            pltpu.VMEM((rows, width), F32),
+            pltpu.VMEM((rows, width), F32),
+            pltpu.VMEM((2 * 2 * DEPTH, STRETCH, width), BF),
+            pltpu.VMEM((2, heads * STRETCH, hd), BF),
+            pltpu.VMEM((2, heads * STRETCH, hd), BF),
+            pltpu.VMEM((2 * 2 * DEPTH, STRETCH, width), BF),
+            pltpu.VMEM((span, width), BF),
+            pltpu.VMEM((span, heads * STRETCH), F32),
+            pltpu.VMEM((span, heads * STRETCH), F32),
+            pltpu.VMEM((2, SPAN + 2, STRETCH, width), F32),
+            pltpu.VMEM((rows, heads * hd), BF),
             pltpu.VMEM((DEPTH, n, hd, hd), BF),
+            pltpu.VMEM((DEPTH, rows, width), BF),
             pltpu.VMEM((DEPTH, rows, width), BF),
             pltpu.VMEM((2, 4, rows, width), BF),
             pltpu.VMEM((2, 4, rows, width), BF),
@@ -697,9 +671,18 @@
             pltpu.VMEM((2, 4, n, hd - FLAT_ROWS, hd), BF),
             pltpu.VMEM((DEPTH, FLAT_ROWS, hd), BF),
             pltpu.VMEM((n, hd - FLAT_ROWS, hd), BF),
+            dma((SENDS,)),
             dma((n,)),
             dma((n,)),
-            dma((WEIGHT_SENDS,)),
+            dma((n,)),
+            dma((2,)),
+            dma((2 * heads,)),
+            dma((2 * heads,)),
+            dma((1,)),
+            dma((2, n, 2)),
+            dma((1,)),
+            dma((2 * DEPTH, 2)),
+            dma((2 * DEPTH,)),
             dma((DEPTH,)),
             dma((2, 4, 2)),
             dma((2,)),
@@ -714,23 +697,12 @@
             dma((DEPTH,)),
         ],
         compiler_params=pltpu.CompilerParams(
-            collective_id=1, has_side_effects=True, vmem_limit_bytes=VMEM_LIMIT
+            collective_id=0, has_side_effects=True, vmem_limit_bytes=VMEM_LIMIT
         ),
-        name="weights",
-    )(part, hidden, hidden_other)
-
-
-def on_device(hidden_in, queries, grad_out, w_key, w_value, stretch_order, doc_lengths):
-    hidden = hidden_in[0]
-    rows, hd = hidden.shape[0], w_key.shape[1]
-    kv, hidden_other = project(hidden, w_key, w_value)
-    ctx = lax.axis_index("ctx").astype(jnp.int32).reshape(1)
-    query_grad, part = attend(
-        stretch_order, doc_lengths[0], ctx, kv.reshape(-1, 2 * hd), queries[0], grad_out[0]
-    )
-    sums = weight_grads(part.reshape(kv.shape), hidden, hidden_other)
-
-    return query_grad[None], sums[0].astype(F32), sums[1].astype(F32)
+        name="kv_backward",
+    )(hidden, queries[0], grad_out[0], w_key, w_value, stretch_order, stored_at, doc_lengths[0])
+    query_grad, key_sums, value_sums = finish(query_grad, sums)
+    return query_grad[None], key_sums, value_sums
 
 
 def solution(mesh):

time: 132 us -> 125 us (0.947)
  Pallas kernels: 129 us -> 123 us
    pallas_call x3 -> x2, Pallas kernels: 129 us -> 123 us  [the longest x1 120 us: on_device(): pl.pallas_call(kernel, out_shape=(jax.ShapeDtypeStruct((rows, heads * hd)...]
    convert_element_type x1 -> x0, other arithmetic: 2.07 us -> none  [on_device(): return (query_grad[None], sums[0].astype(F32), sums[1].astype(F32))]
where the time goes in v3:
time: 125 us
  Pallas kernels  123 us (98%)
  other arithmetic  1.28 us (1%)
    pallas_call x1, Pallas kernels, on_device(): pl.pallas_call(kernel, out_shape=(jax.ShapeDtypeStruct((rows, heads * hd)...  120 us
    pallas_call x1, Pallas kernels, finish(): pl.pallas_call(finish_kernel, grid=(steps,), out_shape=(jax.ShapeDtypeStr...  3.44 us

profile of v3, /device:TPU:1, one launch (start us, length us, event | category | flops | bytes accessed | tf_op | source)
XLA Modules:
  0.0 125.0 jit_solution(1244596903594087647)
XLA Ops:
  0.6 1.3 %select_reduce_fusion.where_ref = s32[32]{0:T(128)} fusion(s32[32]{0:T(128)} %order_ref.1), kind=kLoop, calls=%fused_computation | loop fusion | flops 3040 | bytes 256 | tf_op jit(solution)/shard_map/reduce_sum | solution.py:634
  1.9 119.6 %kv_backward.1 = (bf16[192,1024]{1,0:T(8,128)(2,1)}, bf16[2,1024,128]{2,1,0:T(8,128)(2,1)}) custom-call(bf16[192,16384]{1,0:T(8,128)(2,1)} %bitcast.5, bf16[192,1024]{1,0:T(8,128)(2,1)} %bitcast.6, bf16[192,1024]{1,0:T(8,128)(2,1)} %bitcast.7, bf16[1024,128]{1,0:T(8,128)(2,1)} %wk_ref.1, bf16[1024,128]{1,0:T(8,128)(2,1)} %wv_ref.1, s32[32]{0:T(128)} %order_ref.1, ...), custom_call_target="tpu_custom_call" | custom-call | tf_op jit(solution)/shard_map/kv_backward/pallas_call | solution.py:637
  121.6 3.4 %finish.1 = (bf16[192,1024]{1,0:T(8,128)(2,1)}, f32[1024,128]{1,0:T(8,128)}, f32[1024,128]{1,0:T(8,128)}) custom-call(bf16[192,1024]{1,0:T(8,128)(2,1)} %get-tuple-element.8.dq_ref, bf16[2,1024,128]{2,1,0:T(8,128)(2,1)} %get-tuple-element.9.sums_ref), custom_call_target="tpu_custom_call" | custom-call | tf_op jit(solution)/shard_map/finish/pallas_call | solution.py:611

commit v4 on v3

--- a/solution.py
+++ b/solution.py
@@ -34,6 +34,9 @@
 
     def along_z(self, d):
         return (self.dp, lax.rem(self.z + d, DEPTH) * 2 + self.core)
+
+    def across(self, d):
+        return (self.dp, lax.rem(self.z + d, DEPTH) * 2 + 1 - self.core)
 
     def along(self, axis, d):
         if axis == 0:
@@ -85,15 +88,15 @@
     ).wait_recv()
 
 
-SENDS = 2 * 20 + 1 + 14 + 8 + 8 + 14 + 2 + 32 + 8 + 14 + 7 + 15 + 7 + 8
+SENDS = 2 * 20 + 1 + 14 + 2 + 7 + 8 + 14 + 2 + 32 + 8 + 14 + 7 + 15 + 7 + 8
 
 
 def kernel(
-    hid_ref, q_ref, g_ref, wk_ref, wv_ref, order_ref, where_ref, lens_ref,
+    hid_ref, q_ref, g_ref, wk_ref, wv_ref, order_ref, lens_ref,
     dq_ref, out_ref,
-    hbuf, wbuf, acc, pin, pout, kv_ref, qs, gs, kp, kw, scores, dprobs, sums, dqs,
+    hbuf, wbuf, acc, pin, pout, kv_ref, where_ref, qs, gs, kp, kw, scores, dprobs, sums, dqs,
     tb, rout, rbuf, zin, zout, gbuf, gt, pr0, pr1, qr0, qr1, cin, zr, xr,
-    s_sem, own_sem, hs_sem, hr_sem, wo_sem, q_sem, go_sem, dq_sem, w_sem, p_sem, z_sem, c_sem,
+    s_sem, own_sem, hs_sem, hr_sem, wo_sem, q_sem, go_sem, dq_sem, w_sem, p_sem, z_sem, c_sem, e_sem,
     d1_sem, d2_sem, d3_sem, p0_sem, p1_sem, q0_sem, q1_sem, n_sem, f_sem, x_sem, g_sem, b_sem,
 ):
     heads = q_ref.shape[1] // wk_ref.shape[1]
@@ -140,6 +143,8 @@
     def _(i):
         h_copies(slot_of(me.x + lax.rem(i, SIDE), me.y + lax.div(i, SIDE)))[0].start()
 
+    for copy in w_own:
+        copy.wait()
     all_here()
     send = Sender(s_sem)
 
@@ -162,19 +167,17 @@
 
     for d in (ahead, back):
         for h in (0, 1):
-            send(w_refs[h], wbuf.at[h, me.dp], w_sem.at[h, me.dp, 0], me.along(h, d))
+            w_send(h, me.dp, h, d)
 
     for d in (ahead, back):
         for h in (0, 1):
-            send(w_refs[h], wbuf.at[h, me.dp], w_sem.at[h, me.dp, 0], me.along(1 - h, d))
+            w_send(h, me.dp, 1 - h, d)
 
     @pl.loop(0, n)
     def _(i):
         h_copies(slot_of(me.x + lax.rem(i, SIDE), me.y + lax.div(i, SIDE)))[1].start()
 
     acc[...] = jnp.zeros_like(acc)
-    for copy in w_own:
-        copy.wait()
 
     def compute(dx, dy):
         s = slot_of(me.x + dx, me.y + dy)
@@ -286,6 +289,15 @@
         z_send(0, down, 1 - first)
     share(0)
 
+    n_stretch = order_ref.shape[0]
+
+    @pl.loop(0, n_stretch)
+    def _(i):
+        at = jnp.int32(0)
+        for b in range(n_stretch):
+            at = jnp.where(order_ref[b] == i, b, at)
+        where_ref[i] = at
+
     for k in (1, 2, 3):
         for first in (0, 1):
             z_wait(DEPTH - k, first)
@@ -294,17 +306,21 @@
             z_wait(k, 1 - first)
             if k < 3 or first == 0:
                 z_send(k, down, 1 - first)
+        if k == 3:
+            for d, step, part in ((DEPTH - 3, up, 0), (3, down, 1)):
+                ref = z_part(d, part)
+                send(ref, ref, e_sem.at[part], me.across(step))
         share(DEPTH - k)
         share(k)
     z_wait(4, 0)
     z_wait(4, 1)
-    share(4)
-
-    @pl.loop(0, DEPTH)
-    def _(i):
-        other = i * 2 + 1 - me.core
-        arrived(kv_ref.at[kv_block(other)], c_sem.at[other], me)
-
+    for d in range(DEPTH):
+        other = lax.rem(me.z + d, DEPTH) * 2 + 1 - me.core
+        if d == 4:
+            for part in (0, 1):
+                arrived(kv_ref.at[other * 2 + part], e_sem.at[part], me)
+        else:
+            arrived(kv_ref.at[kv_block(other)], c_sem.at[other], me)
 
     factor = math.log2(math.e) / math.sqrt(hd)
     scale = 1.0 / math.sqrt(hd)
@@ -604,7 +620,7 @@
 
 
 def finish(query_grad, sums):
-    steps = 4
+    steps = 2
     (rows, width), (_, depth, hd) = query_grad.shape, sums.shape
     dq_spec = pl.BlockSpec((rows // steps, width), lambda i: (i, 0))
     out_spec = pl.BlockSpec((depth // steps, hd), lambda i: (i, 0))
@@ -630,8 +646,6 @@
     width, span = 2 * hd, SPAN * STRETCH
     heads = queries.shape[2] // hd
     groups = DEPTH // 2
-    every = jnp.arange(stretch_order.shape[0], dtype=jnp.int32)
-    stored_at = jnp.sum(jnp.where(stretch_order[None, :] == every[:, None], every[None, :], 0), axis=1)
     dma = pltpu.SemaphoreType.DMA
     smem, hbm = pl.BlockSpec(memory_space=pltpu.SMEM), pl.BlockSpec(memory_space=pl.ANY)
     query_grad, sums = pl.pallas_call(
@@ -640,7 +654,7 @@
             jax.ShapeDtypeStruct((rows, heads * hd), BF),
             jax.ShapeDtypeStruct((2, 2 * cols, hd), BF),
         ),
-        in_specs=[hbm] * 5 + [smem] * 3,
+        in_specs=[hbm] * 5 + [smem] * 2,
         out_specs=(hbm, pl.BlockSpec(memory_space=pltpu.VMEM)),
         scratch_shapes=[
             pltpu.VMEM((n, 2 * rows, cols), BF),
@@ -649,6 +663,7 @@
             pltpu.VMEM((rows, width), F32),
             pltpu.VMEM((rows, width), F32),
             pltpu.VMEM((2 * 2 * DEPTH, STRETCH, width), BF),
+            pltpu.SMEM(stretch_order.shape, jnp.int32),
             pltpu.VMEM((2, heads * STRETCH, hd), BF),
             pltpu.VMEM((2, heads * STRETCH, hd), BF),
             pltpu.VMEM((2 * 2 * DEPTH, STRETCH, width), BF),
@@ -683,6 +698,7 @@
             dma((1,)),
             dma((2 * DEPTH, 2)),
             dma((2 * DEPTH,)),
+            dma((2,)),
             dma((DEPTH,)),
             dma((2, 4, 2)),
             dma((2,)),
@@ -700,7 +716,7 @@
             collective_id=0, has_side_effects=True, vmem_limit_bytes=VMEM_LIMIT
         ),
         name="kv_backward",
-    )(hidden, queries[0], grad_out[0], w_key, w_value, stretch_order, stored_at, doc_lengths[0])
+    )(hidden, queries[0], grad_out[0], w_key, w_value, stretch_order, doc_lengths[0])
     query_grad, key_sums, value_sums = finish(query_grad, sums)
     return query_grad[None], key_sums, value_sums
 

time: 125 us -> 123 us (0.984)
  other arithmetic: 1.28 us -> 0 us
    reduce_sum x1 -> x0, other arithmetic: 1.28 us -> none  [on_device(): jnp.sum(jnp.where(stretch_order[None, :] == every[:, None], every[None, :...]
where the time goes in v4:
time: 123 us
  Pallas kernels  122 us (99%)
    pallas_call x1, Pallas kernels, on_device(): pl.pallas_call(kernel, out_shape=(jax.ShapeDtypeStruct((rows, heads * hd)...  120 us

profile of v4, /device:TPU:1, one launch (start us, length us, event | category | flops | bytes accessed | tf_op | source)
XLA Modules:
  0.0 122.8 jit_solution(5058692394202059749)
XLA Ops:
  0.6 119.9 %kv_backward.1 = (bf16[192,1024]{1,0:T(8,128)(2,1)}, bf16[2,1024,128]{2,1,0:T(8,128)(2,1)}) custom-call(bf16[192,16384]{1,0:T(8,128)(2,1)} %bitcast.5, bf16[192,1024]{1,0:T(8,128)(2,1)} %bitcast.6, bf16[192,1024]{1,0:T(8,128)(2,1)} %bitcast.7, bf16[1024,128]{1,0:T(8,128)(2,1)} %wk_ref.1, bf16[1024,128]{1,0:T(8,128)(2,1)} %wv_ref.1, s32[32]{0:T(128)} %order_ref.1, ...), custom_call_target="tpu_custom_call" | custom-call | tf_op jit(solution)/shard_map/kv_backward/pallas_call | solution.py:651
  120.6 2.2 %finish.1 = (bf16[192,1024]{1,0:T(8,128)(2,1)}, f32[1024,128]{1,0:T(8,128)}, f32[1024,128]{1,0:T(8,128)}) custom-call(bf16[192,1024]{1,0:T(8,128)(2,1)} %get-tuple-element.8.dq_ref, bf16[2,1024,128]{2,1,0:T(8,128)(2,1)} %get-tuple-element.9.sums_ref), custom_call_target="tpu_custom_call" | custom-call | tf_op jit(solution)/shard_map/finish/pallas_call | solution.py:627

commit v5 on v4

--- a/solution.py
+++ b/solution.py
@@ -94,7 +94,7 @@
 def kernel(
     hid_ref, q_ref, g_ref, wk_ref, wv_ref, order_ref, lens_ref,
     dq_ref, out_ref,
-    hbuf, wbuf, acc, pin, pout, kv_ref, where_ref, qs, gs, kp, kw, scores, dprobs, sums, dqs,
+    hbuf, wbuf, acc, pin, pout, kv_ref, where_ref, qs, gs, kw, scores, dprobs, sums, dqs,
     tb, rout, rbuf, zin, zout, gbuf, gt, pr0, pr1, qr0, qr1, cin, zr, xr,
     s_sem, own_sem, hs_sem, hr_sem, wo_sem, q_sem, go_sem, dq_sem, w_sem, p_sem, z_sem, c_sem, e_sem,
     d1_sem, d2_sem, d3_sem, p0_sem, p1_sem, q0_sem, q1_sem, n_sem, f_sem, x_sem, g_sem, b_sem,
@@ -335,10 +335,6 @@
         for copy in q_copies(i):
             copy.wait()
 
-    @pl.loop(0, where_ref.shape[0])
-    def _(i):
-        kp[i] = kv_ref[where_ref[i]]
-
     for t in (0, 1):
         for at in (0, SPAN + 1):
             sums[t, at] = jnp.zeros((STRETCH, 2 * hd), F32)
@@ -350,7 +346,7 @@
 
         @pl.loop(0, SPAN)
         def _(i):
-            kw[pl.ds(pl.multiple_of(i * STRETCH, STRETCH), STRETCH)] = kp[first + i]
+            kw[pl.ds(pl.multiple_of(i * STRETCH, STRETCH), STRETCH)] = kv_ref[where_ref[first + i]]
 
         spot = place * STRETCH + lax.rem(lax.broadcasted_iota(jnp.int32, (1, width), 1), STRETCH)
         low = jnp.zeros_like(spot)
@@ -666,7 +662,6 @@
             pltpu.SMEM(stretch_order.shape, jnp.int32),
             pltpu.VMEM((2, heads * STRETCH, hd), BF),
             pltpu.VMEM((2, heads * STRETCH, hd), BF),
-            pltpu.VMEM((2 * 2 * DEPTH, STRETCH, width), BF),
             pltpu.VMEM((span, width), BF),
             pltpu.VMEM((span, heads * STRETCH), F32),
             pltpu.VMEM((span, heads * STRETCH), F32),

time: 123 us -> 123 us (level)
  no operation moved by 1% of the time
where the time goes in v5:
time: 123 us
  Pallas kernels  122 us (99%)
    pallas_call x1, Pallas kernels, on_device(): pl.pallas_call(kernel, out_shape=(jax.ShapeDtypeStruct((rows, heads * hd)...  120 us

profile of v5, /device:TPU:1, one launch (start us, length us, event | category | flops | bytes accessed | tf_op | source)
XLA Modules:
  0.0 122.6 jit_solution(13067480413780424584)
XLA Ops:
  0.6 119.8 %kv_backward.1 = (bf16[192,1024]{1,0:T(8,128)(2,1)}, bf16[2,1024,128]{2,1,0:T(8,128)(2,1)}) custom-call(bf16[192,16384]{1,0:T(8,128)(2,1)} %bitcast.5, bf16[192,1024]{1,0:T(8,128)(2,1)} %bitcast.6, bf16[192,1024]{1,0:T(8,128)(2,1)} %bitcast.7, bf16[1024,128]{1,0:T(8,128)(2,1)} %wk_ref.1, bf16[1024,128]{1,0:T(8,128)(2,1)} %wv_ref.1, s32[32]{0:T(128)} %order_ref.1, ...), custom_call_target="tpu_custom_call" | custom-call | tf_op jit(solution)/shard_map/kv_backward/pallas_call | solution.py:647
  120.4 2.2 %finish.1 = (bf16[192,1024]{1,0:T(8,128)(2,1)}, f32[1024,128]{1,0:T(8,128)}, f32[1024,128]{1,0:T(8,128)}) custom-call(bf16[192,1024]{1,0:T(8,128)(2,1)} %get-tuple-element.8.dq_ref, bf16[2,1024,128]{2,1,0:T(8,128)(2,1)} %get-tuple-element.9.sums_ref), custom_call_target="tpu_custom_call" | custom-call | tf_op jit(solution)/shard_map/finish/pallas_call | solution.py:623
